TPU v7x, 512 devices: a whole 4x8x8 slice. The times are simulated.
512 devices in a mesh: ax: 64 (over x, y_lo, z), az: 8 (over y_hi, core).
Axes of the slice: x: 4, y: 8 (y_hi: 4, y_lo: 2; y = y_hi * 2 + y_lo), z: 8, core: 2. Of those that a mesh axis runs over, the one named last changes fastest.
Arguments:
- layer_input: bfloat16 [64, 128, 128, 128], P(None, 'ax', 'az'), may hold values from -6 to 6
- pre_act: bfloat16 [64, 128, 128, 128], P(None, 'ax', 'az'), may hold values from -6 to 6
- out_grad: bfloat16 [64, 128, 128, 128], P(None, 'ax', 'az'), may hold values from -6 to 6
- point_weight: bfloat16 [64, 64], replicated, may hold values from -0.75 to 0.75
- spec_weight: bfloat16 [512, 32, 4096], P(('az', 'ax')), may hold values from -0.75 to 0.75
- saved_coeffs: bfloat16 [512, 2048], P(('az', 'ax')), may hold values from -0.625 to 0.625
Outputs:
- input_grad: bfloat16 [64, 128, 128, 128], P(None, 'ax', 'az')
- point_grad: float32 [64, 64], replicated
- bias_grad: float32 [64], replicated
- spec_grad: bfloat16 [512, 32, 4096], P(('az', 'ax'))
All inputs are finite; a program needn't handle non-finite values.
Results may differ from a plain program's by a relative error of at most 0.012.
Values may be sent and summed in bfloat16 or wider, within the bound.
No kernel may reach another device: no remote copies, remote signals or barrier semaphores. Data moves between devices by JAX's collectives and lax.ppermute only.
A program may use at most 64 MiB of HBM per device.

v0:
```python
import math

import jax
import jax.numpy as jnp
from jax import lax
from jax.sharding import PartitionSpec as P

CH = 64
MX = 32
MT = 16
MR = 16


def gelu_slope(values):
    density = jnp.exp(-0.5 * values * values) * (1.0 / math.sqrt(2.0 * math.pi))
    return 0.5 * (1.0 + lax.erf(values * (1.0 / math.sqrt(2.0)))) + values * density


def cosine_table(extent, wanted, offset, height):
    places = (offset + jnp.arange(height)).astype(jnp.float32) + 0.5
    orders = jnp.arange(wanted).astype(jnp.float32)
    scaled = math.sqrt(2.0 / extent) * jnp.cos(math.pi * places[:, None] * orders[None, :] / extent)
    scaled = jnp.where(orders[None, :] == 0.0, scaled * (1.0 / math.sqrt(2.0)), scaled)
    return scaled.astype(jnp.bfloat16)


def cycle_table(extent, half_modes, offset, height):
    places = (offset + jnp.arange(height)).astype(jnp.float32) + 0.5
    angles = 2.0 * math.pi * places / extent
    orders = jnp.arange(half_modes).astype(jnp.float32)
    cosines = math.sqrt(2.0 / extent) * jnp.cos(angles[:, None] * orders[None, :])
    cosines = jnp.where(orders[None, :] == 0.0, cosines * (1.0 / math.sqrt(2.0)), cosines)
    sine_part = math.sqrt(2.0 / extent) * jnp.sin(angles[:, None] * (orders[None, :] + 1.0))
    return jnp.concatenate([cosines, sine_part], axis=1).astype(jnp.bfloat16)


def per_device(layer_input, pre_act, out_grad, point_weight, spec_weight, saved_coeffs):
    axial_devices = lax.axis_size("ax")
    cycle_devices = lax.axis_size("az")
    slab_length = layer_input.shape[1]
    sector_length = layer_input.shape[2]
    radial_length = layer_input.shape[3]
    axial_total = slab_length * axial_devices
    cycle_total = sector_length * cycle_devices
    cells_total = axial_total * cycle_total * radial_length
    synth_gain = math.sqrt(axial_total * cycle_total * radial_length / (2.0 * MX * MT * MR))
    modes_here = 2 * MT // cycle_devices
    pairs_group = modes_here * MR
    pairs_here = spec_weight.shape[0]
    radial_table = cosine_table(radial_length, MR, 0, radial_length)
    cycle_local = cycle_table(cycle_total, MT, lax.axis_index("az") * sector_length, sector_length)
    axial_local = cosine_table(axial_total, MX, lax.axis_index("ax") * slab_length, slab_length)
    activation_slope = gelu_slope(pre_act.astype(jnp.float32))
    grad_pre = (out_grad.astype(jnp.float32) * activation_slope).astype(jnp.bfloat16)
    point_local = jnp.einsum(
        "ixtr,oxtr->io", layer_input, grad_pre, preferred_element_type=jnp.float32
    )
    bias_local = jnp.sum(grad_pre.astype(jnp.float32), axis=(1, 2, 3))
    point_sum, bias_sum = lax.psum((point_local, bias_local), ("ax", "az"))
    norm_scale = 1.0 / math.sqrt(cells_total)
    point_grad = point_sum * norm_scale
    bias_grad = bias_sum * norm_scale
    point_part = jnp.einsum(
        "io,oxtr->ixtr", point_weight, grad_pre, preferred_element_type=jnp.float32
    )
    radial_coef = jnp.einsum(
        "ixtr,rk->ixtk", grad_pre, radial_table, preferred_element_type=jnp.float32
    )
    cycle_wide = cycle_local.astype(jnp.float32)
    columns = cycle_wide
    mode_sums = lax.psum_scatter(
        jnp.einsum("ixtk,tm->mkxi", radial_coef, columns, precision=lax.Precision.HIGHEST),
        "az",
        scatter_dimension=0,
        tiled=True,
    )
    spectral_in = mode_sums.astype(jnp.bfloat16).reshape(pairs_group, slab_length, CH)
    axial_sum = lax.psum_scatter(
        jnp.einsum("pxi,xk->pki", spectral_in, axial_local, preferred_element_type=jnp.float32),
        "ax",
        scatter_dimension=0,
        tiled=True,
    )
    mode_grad = (synth_gain * axial_sum).astype(jnp.bfloat16)
    mixing = spec_weight.reshape(pairs_here, MX, CH, CH)
    coef_grad = jnp.einsum(
        "pkio,pko->pki", mixing, mode_grad, preferred_element_type=jnp.float32
    ).astype(jnp.bfloat16)
    saved_modes = saved_coeffs.reshape(pairs_here, MX, CH).astype(jnp.float32)
    spec_grad = (
        (saved_modes[:, :, :, None] * mode_grad.astype(jnp.float32)[:, :, None, :])
        .astype(jnp.bfloat16)
        .reshape(pairs_here, MX, CH * CH)
    )
    slab_modes = jnp.einsum(
        "pki,xk->pxi",
        lax.all_gather(coef_grad, "ax", axis=0, tiled=True),
        axial_local,
        preferred_element_type=jnp.float32,
    ).astype(jnp.bfloat16)
    cycle_modes = slab_modes.reshape(modes_here, MR, slab_length, CH)
    columns = cycle_local
    radial_modes = jnp.einsum(
        "mkxi,tm->ixtk",
        lax.all_gather(cycle_modes, "az", axis=0, tiled=True),
        columns,
        preferred_element_type=jnp.float32,
    )
    spectral_part = jnp.einsum(
        "ixtk,rk->ixtr",
        radial_modes,
        radial_table.astype(jnp.float32),
        precision=lax.Precision.HIGHEST,
    )
    input_grad = (spectral_part + point_part).astype(jnp.bfloat16)
    return (input_grad, point_grad, bias_grad, spec_grad)


def solution(mesh):
    return jax.shard_map(
        per_device,
        mesh=mesh,
        in_specs=(
            P(None, "ax", "az", None),
            P(None, "ax", "az", None),
            P(None, "ax", "az", None),
            P(),
            P(("az", "ax"), None, None),
            P(("az", "ax"), None),
        ),
        out_specs=(P(None, "ax", "az", None), P(), P(), P(("az", "ax"), None, None)),
        check_vma=False,
    )
```

profile of v0, /device:TPU:1, one launch (start us, length us, event | category | flops | bytes accessed | tf_op | source)
XLA Modules:
  0.0 561.5 jit_solution(13889702866088393135)
XLA Ops:
  7.2 0.0 copy-start
  7.2 0.0 reduce-scatter.3.cloned.1.call-start
  7.3 2.0 convert_reduce_fusion
  9.3 0.4 fusion.20
  9.7 0.7 copy.22
  10.3 0.1 select_convert_fusion.1
  10.5 0.5 convolution_bitcast_fusion.1
  11.0 1.1 copy.23
  12.1 0.0 reduce-scatter.3.cloned.1.call-update
  12.1 0.0 reduce-scatter.5.cloned.1.call-start
  12.2 44.2 %reduce-scatter.3.cloned.1.call-done = f32[4,16,2,64]{3,1,2,0:T(8,128)} async-done(((f32[32,16,2,64]{3,1,2,0:T(8,128)}), f32[4,16,2,64]{3,1,2,0:T(8,128)}) %reduce-scatter.3.cloned.1.call-update) | async-done | bytes 32784 | tf_op jit(solution)/shard_map/reduce_scatter | solution.py:71
  56.4 0.8 copy.54
  57.2 1.4 convolution_bitcast_fusion
  58.7 0.0 copy-start.1
  58.7 0.0 reduce-scatter.5.cloned.1.call-update
  58.7 0.9 copy-done.1
  59.6 0.0 copy-start.3
  59.6 0.5 reshape.114
  60.2 0.2 copy-done.3
  60.4 0.1 reshape.116
  60.4 0.0 copy-done
  60.4 0.6 convolution_bitcast_fusion.3
  61.1 101.6 %all-reduce = (f32[64,64]{0,1:T(8,128)S(1)}, f32[64]{0:T(128)S(1)}) all-reduce(f32[64,64]{0,1:T(8,128)S(1)} %convolution_bitcast_fusion.3, f32[64]{0:T(128)S(1)} %get-tuple-element.18), channel_id=1, replica_groups=mesh['ax'=64,'az'=8] {'ax','az'}, use_global_device_ids=true, to_apply=%region_2.3 | all-reduce | flops 4160 | bytes 33280 | tf_op jit(solution)/shard_map/psum | solution.py:59
  162.7 0.0 copy-start.2
  162.7 0.7 copy.33
  163.4 0.5 broadcast_multiply_fusion.1
  163.9 0.0 copy-done.2
  163.9 0.3 fusion.11
  164.2 162.4 %reduce-scatter.5.cloned.1.call-done = f32[1,32,64]{2,1,0:T(8,128)} async-done(((f32[64,32,64]{2,1,0:T(8,128)}), f32[1,32,64]{2,1,0:T(8,128)}) %reduce-scatter.5.cloned.1.call-update) | async-done | bytes 8208 | tf_op jit(solution)/shard_map/reduce_scatter | solution.py:78
  326.6 0.7 bitcast_convert_fusion
  327.3 0.4 fusion.16
  327.7 127.6 %all-gather = bf16[2048,64]{1,0:T(8,128)(2,1)S(1)} all-gather(bf16[32,64]{1,0:T(8,128)(2,1)S(1)} %convert_element_type.141), channel_id=2, replica_groups=mesh['ax'=64,'az'=8] {'ax'}, dimensions={0}, use_global_device_ids=true | all-gather | bytes 266240 | tf_op jit(solution)/shard_map/all_gather | solution.py:97
  455.3 0.3 convolution_convert_fusion
  455.6 94.4 %all_gather.7 = bf16[32,16,2,64]{3,1,2,0:T(8,128)(2,1)S(1)} all-gather(bf16[4,16,2,64]{3,1,2,0:T(8,128)(2,1)S(1)} %copy.26), channel_id=1, replica_groups=mesh['ax'=64,'az'=8] {'az'}, dimensions={0}, use_global_device_ids=true | all-gather | bytes 147456 | tf_op jit(solution)/shard_map/all_gather | solution.py:105
  550.0 0.2 convolution_bitcast_fusion.2
  550.2 0.9 copy.28
  551.2 0.3 multiply_convert_fusion
  551.5 1.2 convert_element_type.150
  552.7 2.0 fusion
  (11 shorter events, 0.1 us)
Async XLA Ops:
  7.2 53.3 %copy-start = (bf16[64,2,16,128]{3,2,1,0:T(8,128)(2,1)S(1)}, bf16[64,2,16,128]{3,2,1,0:T(8,128)(2,1)}, u32[]{:S(2)}) copy-start(bf16[64,2,16,128]{3,2,1,0:T(8,128)(2,1)} %param.6) | copy-start | bytes 1572868
  7.2 49.2 %reduce-scatter.3.cloned.1.call-start = ((), (), s32[]{:S(2)}) async-start(), calls=%async_computation.2 | async-start | bytes 589824 | tf_op jit(solution)/shard_map/reduce_scatter | solution.py:71
  12.1 314.5 %reduce-scatter.5.cloned.1.call-start = ((), (), s32[]{:S(2)}) async-start(), calls=%async_computation.3 | async-start | bytes 1064960 | tf_op jit(solution)/shard_map/reduce_scatter | solution.py:78
  58.7 0.9 copy-start.1
  59.6 0.7 copy-start.3
  162.7 1.2 copy-start.2
Sparse Core Ops, SparseCore 0:
  12.2 44.1 reduce-scatter.2
  59.4 267.1 reduce-scatter.4
where the time goes:
time: 562 us; the launch traced here: 561 us
  blocking collectives  324 us (58%)
  waiting for transfers between devices  207 us (37%)
  between operations  14.2 us (3%)
  local copies, waits for them, and re-layouts  7.12 us (1%)
  matrix products  6.08 us (1%)
    reduce_scatter x1, waiting for transfers between devices, per_device(): lax.psum_scatter(jnp.einsum('pxi,xk->pki', spectral_in, axial_local, pref...  162 us
    all_gather x1, blocking collectives, per_device(): lax.all_gather(coef_grad, 'ax', axis=0, tiled=True)  128 us
    psum x1, blocking collectives, per_device(): point_sum, bias_sum = lax.psum((point_local, bias_local), ('ax', 'az'))  102 us
    all_gather x1, blocking collectives, per_device(): lax.all_gather(cycle_modes, 'az', axis=0, tiled=True)  94.4 us
    reduce_scatter x1, waiting for transfers between devices, per_device(): lax.psum_scatter(jnp.einsum('ixtk,tm->mkxi', radial_coef, columns, precis...  44.2 us
  transfers between devices with their start and end apart: 2, of which 2 were waited for; matrix products, arithmetic and copies ran while one was open for 0% of the time, Pallas kernels for 0%

commit v1 on v0

v1 whole, which is shorter than its diff:
```python
import math

import jax
import jax.numpy as jnp
from jax import lax
from jax.sharding import PartitionSpec as P

CH = 64
MX = 32
MT = 16
MR = 16


def gelu_slope(values):
    density = jnp.exp(-0.5 * values * values) * (1.0 / math.sqrt(2.0 * math.pi))
    return 0.5 * (1.0 + lax.erf(values * (1.0 / math.sqrt(2.0)))) + values * density


def cosine_table(extent, wanted, offset, height):
    places = (offset + jnp.arange(height)).astype(jnp.float32) + 0.5
    orders = jnp.arange(wanted).astype(jnp.float32)
    scaled = math.sqrt(2.0 / extent) * jnp.cos(math.pi * places[:, None] * orders[None, :] / extent)
    scaled = jnp.where(orders[None, :] == 0.0, scaled * (1.0 / math.sqrt(2.0)), scaled)
    return scaled.astype(jnp.bfloat16)


def cycle_table(extent, half_modes, offset, height):
    places = (offset + jnp.arange(height)).astype(jnp.float32) + 0.5
    angles = 2.0 * math.pi * places / extent
    orders = jnp.arange(half_modes).astype(jnp.float32)
    cosines = math.sqrt(2.0 / extent) * jnp.cos(angles[:, None] * orders[None, :])
    cosines = jnp.where(orders[None, :] == 0.0, cosines * (1.0 / math.sqrt(2.0)), cosines)
    sine_part = math.sqrt(2.0 / extent) * jnp.sin(angles[:, None] * (orders[None, :] + 1.0))
    return jnp.concatenate([cosines, sine_part], axis=1).astype(jnp.bfloat16)


def two_parts(values):
    high = lax.reduce_precision(values, 8, 7)
    return high.astype(jnp.bfloat16), (values - high).astype(jnp.bfloat16)


def per_device(layer_input, pre_act, out_grad, point_weight, spec_weight, saved_coeffs):
    axial_devices = lax.axis_size("ax")
    cycle_devices = lax.axis_size("az")
    devices = axial_devices * cycle_devices
    slab_length = layer_input.shape[1]
    sector_length = layer_input.shape[2]
    radial_length = layer_input.shape[3]
    axial_total = slab_length * axial_devices
    cycle_total = sector_length * cycle_devices
    cells_total = axial_total * cycle_total * radial_length
    synth_gain = math.sqrt(cells_total / (2.0 * MX * MT * MR))
    norm_scale = 1.0 / math.sqrt(cells_total)
    row = slab_length * CH
    sums_total = CH * CH + CH
    share = -(-sums_total // devices)
    radial_table = cosine_table(radial_length, MR, 0, radial_length)
    axial_table = cosine_table(axial_total, MX, 0, axial_total)
    cycle_local = cycle_table(cycle_total, MT, lax.axis_index("az") * sector_length, sector_length)

    grad_pre = (out_grad.astype(jnp.float32) * gelu_slope(pre_act.astype(jnp.float32))).astype(jnp.bfloat16)
    point_local = jnp.einsum("ixtr,oxtr->io", layer_input, grad_pre, preferred_element_type=jnp.float32)
    bias_local = jnp.sum(grad_pre.astype(jnp.float32), axis=(1, 2, 3))
    radial_coef = jnp.einsum(
        "ixtr,rk->ixtk", grad_pre, radial_table, preferred_element_type=jnp.float32
    ).astype(jnp.bfloat16)
    modes = jnp.einsum("ixtk,tm->mkxi", radial_coef, cycle_local, preferred_element_type=jnp.float32)
    modes = modes.astype(jnp.bfloat16).reshape(devices, row)
    sums = jnp.concatenate([point_local.reshape(-1), bias_local, jnp.zeros(share * devices - sums_total, jnp.float32)])
    high, low = two_parts(sums.reshape(devices, share))
    sums_row = jnp.pad(jnp.concatenate([high, low], axis=1), ((0, 0), (0, row - 2 * share)))
    sent = jnp.stack([modes, sums_row], axis=1)
    got = lax.all_to_all(sent, ("az", "ax"), 0, 0, tiled=True)

    spectral_in = jnp.sum(
        got[:, 0].reshape(cycle_devices, axial_total, CH).astype(jnp.float32), axis=0
    ).astype(jnp.bfloat16)
    sums_here = jnp.sum(got[:, 1, : 2 * share].astype(jnp.float32), axis=0)
    sums_here = (sums_here[:share] + sums_here[share:]) * norm_scale
    mode_grad = synth_gain * jnp.einsum(
        "xi,xk->ki", spectral_in, axial_table, preferred_element_type=jnp.float32
    )
    mode_grad = mode_grad.astype(jnp.bfloat16)
    mixing = spec_weight.reshape(MX, CH, CH)
    coef_grad = jnp.einsum("kio,ko->ki", mixing, mode_grad, preferred_element_type=jnp.float32).astype(jnp.bfloat16)
    saved_modes = saved_coeffs.reshape(MX, CH).astype(jnp.float32)
    spec_grad = (
        (saved_modes[:, :, None] * mode_grad.astype(jnp.float32)[:, None, :])
        .astype(jnp.bfloat16)
        .reshape(1, MX, CH * CH)
    )
    slab_modes = jnp.einsum("ki,xk->xi", coef_grad, axial_table, preferred_element_type=jnp.float32)
    slab_modes = slab_modes.astype(jnp.bfloat16).reshape(1, axial_devices, row)
    slab_modes = jnp.broadcast_to(slab_modes, (cycle_devices, axial_devices, row)).reshape(devices, row)
    high, low = two_parts(sums_here)
    sums_row = jnp.pad(jnp.concatenate([high, low]), (0, row - 2 * share))
    sent = jnp.stack([slab_modes, jnp.broadcast_to(sums_row, (devices, row))], axis=1)
    got = lax.all_to_all(sent, ("az", "ax"), 0, 0, tiled=True)

    cycle_modes = got[:, 0].reshape(2 * MT, MR, slab_length, CH)
    sums_all = got[:, 1, :share].astype(jnp.float32) + got[:, 1, share : 2 * share].astype(jnp.float32)
    sums_all = sums_all.reshape(-1)
    point_grad = sums_all[: CH * CH].reshape(CH, CH)
    bias_grad = sums_all[CH * CH : sums_total]
    point_part = jnp.einsum("io,oxtr->ixtr", point_weight, grad_pre, preferred_element_type=jnp.float32)
    radial_modes = jnp.einsum(
        "mkxi,tm->ixtk", cycle_modes, cycle_local, preferred_element_type=jnp.float32
    ).astype(jnp.bfloat16)
    spectral_part = jnp.einsum("ixtk,rk->ixtr", radial_modes, radial_table, preferred_element_type=jnp.float32)
    input_grad = (spectral_part + point_part).astype(jnp.bfloat16)
    return (input_grad, point_grad, bias_grad, spec_grad)


def solution(mesh):
    return jax.shard_map(
        per_device,
        mesh=mesh,
        in_specs=(
            P(None, "ax", "az", None),
            P(None, "ax", "az", None),
            P(None, "ax", "az", None),
            P(),
            P(("az", "ax"), None, None),
            P(("az", "ax"), None),
        ),
        out_specs=(P(None, "ax", "az", None), P(), P(), P(("az", "ax"), None, None)),
        check_vma=False,
    )
```

time: 562 us -> 84.3 us (0.15)
  blocking collectives: 324 us -> 0 us
  waiting for transfers between devices: 207 us -> 31.1 us
  starting transfers between devices: 0.08 us -> 30.8 us
  between operations: 14.2 us -> 0.94 us
    all_gather x2 -> x0, blocking collectives: 222 us -> none  [the longest x1 128 us: per_device(): lax.all_gather(coef_grad, 'ax', axis=0, tiled=True)]
    reduce_scatter x2 -> x0, waiting for transfers between devices: 207 us -> none  [the longest x1 162 us: per_device(): lax.psum_scatter(jnp.einsum('pxi,xk->pki', spectral_in, axial_local, pref...]
    psum x1 -> x0, blocking collectives: 102 us -> none  [per_device(): point_sum, bias_sum = lax.psum((point_local, bias_local), ('ax', 'az'))]
    all_to_all x0 -> x2, waiting for transfers between devices: none -> 31.1 us  [per_device(): got = lax.all_to_all(sent, ('az', 'ax'), 0, 0, tiled=True)]
    all_to_all x0 -> x2, starting transfers between devices: none -> 30.8 us  [per_device(): got = lax.all_to_all(sent, ('az', 'ax'), 0, 0, tiled=True)]
  transfers between devices with their start and end apart: 2 -> 2, of which waited for: 2 -> 2; matrix products, arithmetic and copies ran while one was open for 0% -> 3% of each run, Pallas kernels for 0% -> 0%
where the time goes in v1:
time: 84.3 us; the launch traced here: 84 us
  waiting for transfers between devices  31.1 us (37%)
  starting transfers between devices  30.8 us (37%)
  local copies, waits for them, and re-layouts  11 us (13%)
  other arithmetic  5.26 us (6%)
  matrix products  4.83 us (6%)
  between operations  0.94 us (1%)
    all_to_all x2, waiting for transfers between devices, per_device(): got = lax.all_to_all(sent, ('az', 'ax'), 0, 0, tiled=True)  31.1 us
    all_to_all x2, starting transfers between devices, per_device(): got = lax.all_to_all(sent, ('az', 'ax'), 0, 0, tiled=True)  30.8 us
    reduce_sum x1, other arithmetic, per_device(): bias_local = jnp.sum(grad_pre.astype(jnp.float32), axis=(1, 2, 3))  2.03 us
    add x1, other arithmetic, per_device(): got[:, 1, :share].astype(jnp.float32)  1.84 us
    dot_general x1, matrix products, per_device(): jnp.einsum('ixtk,rk->ixtr', radial_modes, radial_table, preferred_element...  1.7 us
  transfers between devices with their start and end apart: 2, of which 2 were waited for; matrix products, arithmetic and copies ran while one was open for 3% of the time, Pallas kernels for 0%

profile of v1, /device:TPU:1, one launch (start us, length us, event | category | flops | bytes accessed | tf_op | source)
XLA Modules:
  0.0 84.0 jit_solution(16552710718211770201)
XLA Ops:
  0.7 2.0 %convert_reduce_fusion = (f32[64]{0:T(128)S(1)}, bf16[64,2,16,128]{3,2,1,0:T(8,128)(2,1)S(1)}) fusion(bf16[64,2,16,128]{3,2,1,0:T(8,128)(2,1)} %param.7, bf16[64,2,16,128]{3,2,1,0:T(8,128)(2,1)} %param.8), kind=kLoop, calls=%fused_computation.23 | loop fusion | flops 3669952 | bytes 1573120 | tf_op jit(solution)/shard_map/reduce_sum | solution.py:63
  2.7 0.4 convolution_convert_fusion
  3.1 0.6 copy.61
  3.8 0.1 select_convert_fusion.4
  3.9 0.3 fusion.1
  4.2 0.3 copy.62
  4.5 0.1 stack_reshape.6
  4.7 0.6 convolution_bitcast_fusion
  5.3 0.1 copy.65
  5.4 0.1 reshape.103
  5.5 0.1 concatenate.14
  5.5 0.2 reshape.104
  5.8 0.1 copy.66
  5.9 0.1 copy.82
  6.1 1.0 %copy.69 = bf16[512,2,128]{2,1,0:T(2,128)(2,1)} copy(bf16[512,2,128]{2,0,1:T(8,128)(2,1)S(1)} %pad_maximum_fusion) | data formatting | bytes 524288 | tf_op jit(solution)/shard_map/stack | solution.py:72
  7.1 22.2 %all-to-all-start = ((bf16[512,2,128]{2,1,0:T(2,128)(2,1)}), bf16[512,2,128]{2,1,0:T(2,128)(2,1)S(1)}, u32[]{:S(2)}, u32[]{:S(2)}) async-start(bf16[512,2,128]{2,1,0:T(2,128)(2,1)} %copy.69), calls=%async_computation | async-start | bytes 524288 | tf_op jit(solution)/shard_map/all_to_all | solution.py:73
  29.3 0.5 reshape.105
  29.9 16.7 %all-to-all-done = bf16[512,2,128]{2,1,0:T(2,128)(2,1)S(1)} async-done(((bf16[512,2,128]{2,1,0:T(2,128)(2,1)}), bf16[512,2,128]{2,1,0:T(2,128)(2,1)S(1)}, u32[]{:S(2)}, u32[]{:S(2)}) %all-to-all-start) | async-done | bytes 262176 | tf_op jit(solution)/shard_map/all_to_all | solution.py:73
  46.6 0.6 fusion.17
  47.1 0.1 reduce-precision_convert_fusion.1
  47.2 0.7 slice_reduce_fusion.1
  47.9 0.1 reshape_squeeze.6
  48.1 0.1 reduce_sum.31
  48.2 0.5 fusion.52
  48.6 0.4 fusion.21
  49.0 0.4 convolution_convert_fusion.3
  49.4 0.1 copy.70
  49.5 0.1 broadcast_in_dim.55
  49.6 0.1 fusion.34
  49.8 1.0 %copy.71 = bf16[512,2,128]{2,1,0:T(2,128)(2,1)} copy(bf16[512,2,128]{2,0,1:T(8,128)(2,1)S(1)} %pad_maximum_fusion.1) | data formatting | bytes 524288 | tf_op jit(solution)/shard_map/stack | solution.py:97
  50.8 8.7 %all-to-all-start.1 = ((bf16[512,2,128]{2,1,0:T(2,128)(2,1)}), bf16[512,2,128]{2,1,0:T(2,128)(2,1)S(1)}, u32[]{:S(2)}, u32[]{:S(2)}) async-start(bf16[512,2,128]{2,1,0:T(2,128)(2,1)} %copy.71), calls=%async_computation.1 | async-start | bytes 524288 | tf_op jit(solution)/shard_map/all_to_all | solution.py:98
  59.5 0.1 reshape.106
  59.6 0.6 copy-done.2
  60.2 0.3 fusion.12
  60.5 0.3 multiply_convert_fusion
  60.8 1.2 %convert_element_type.197 = bf16[1,32,4096]{2,1,0:T(8,128)(2,1)} reshape(bf16[32,64,64]{2,1,0:T(8,128)(2,1)S(1)} %multiply_convert_fusion) | data formatting | bytes 524288 | tf_op jit(solution)/shard_map/convert_element_type | solution.py:89
  62.0 14.4 %all-to-all-done.1 = bf16[512,2,128]{2,1,0:T(2,128)(2,1)S(1)} async-done(((bf16[512,2,128]{2,1,0:T(2,128)(2,1)}), bf16[512,2,128]{2,1,0:T(2,128)(2,1)S(1)}, u32[]{:S(2)}, u32[]{:S(2)}) %all-to-all-start.1) | async-done | bytes 262176 | tf_op jit(solution)/shard_map/all_to_all | solution.py:98
  76.4 0.7 slice_reduce_fusion
  77.2 0.1 reshape_squeeze.7
  77.3 0.2 fusion.2
  77.6 0.8 copy.73
  78.4 0.5 broadcast.107
  78.9 1.8 %fusion.49 = (f32[512,9]{1,0:T(8,128)S(1)}, f32[512,1,9]{2,1,0:T(1,128)S(1)}) fusion(f32[]{:T(128)} %broadcast.107, bf16[512,2,128]{2,1,0:T(2,128)(2,1)S(1)} %all-to-all-done.1), kind=kLoop, calls=%fused_computation.89 | loop fusion | flops 13824 | bytes 55300 | tf_op jit(solution)/shard_map/add | solution.py:101
  80.7 0.2 add.80
  80.9 0.6 slice.42
  81.5 0.2 add.81
  81.8 0.5 slice.43
  82.3 1.7 %fusion = bf16[64,2,16,128]{3,2,1,0:T(8,128)(2,1)} fusion(bf16[64,2,16,16]{3,2,1,0:T(8,128)(2,1)S(1)} %copy.73, f32[2,16,128,64]{2,3,1,0:T(8,128)S(1)} %fusion.12, f32[16]{0:T(128)S(1)} %iota_convert_fusion.1, f32[128]{0:T(128)S(1)} %add_multiply_fusion.1, pred[16]{0:T(512)(128)(4,1)S(1)} %broadcast_compare_fusion.1), kind=kOutput, calls=%fused_computation.5 | convolution fusion | flops 8925184 | bytes 1638992 | tf_op jit(solution)/shard_map/ixtk,rk->ixtr/dot_general | solution.py:109
  (23 shorter events, 0.2 us)
Async XLA Ops:
  0.6 4.0 %copy-start = (bf16[64,2,16,128]{3,2,1,0:T(8,128)(2,1)S(1)}, bf16[64,2,16,128]{3,2,1,0:T(8,128)(2,1)}, u32[]{:S(2)}) copy-start(bf16[64,2,16,128]{3,2,1,0:T(8,128)(2,1)} %param.6) | copy-start | bytes 1572868
  7.1 22.2 %copy-start.1 = (bf16[1,32,4096]{2,1,0:T(8,128)(2,1)S(1)}, bf16[1,32,4096]{2,1,0:T(8,128)(2,1)}, u32[]{:S(2)}) copy-start(bf16[1,32,4096]{2,1,0:T(8,128)(2,1)} %param.10) | copy-start | bytes 786436
  7.1 39.4 %all-to-all-start = ((bf16[512,2,128]{2,1,0:T(2,128)(2,1)}), bf16[512,2,128]{2,1,0:T(2,128)(2,1)S(1)}, u32[]{:S(2)}, u32[]{:S(2)}) async-start(bf16[512,2,128]{2,1,0:T(2,128)(2,1)} %copy.69), calls=%async_computation | async-start | bytes 524288 | tf_op jit(solution)/shard_map/all_to_all | solution.py:73
  50.8 8.7 %copy-start.3 = (bf16[1,2048]{1,0:T(2,128)(2,1)S(1)}, bf16[1,2048]{1,0:T(2,128)(2,1)}, u32[]{:S(2)}) copy-start(bf16[1,2048]{1,0:T(2,128)(2,1)} %param.11) | copy-start | bytes 12292
  50.8 25.7 %all-to-all-start.1 = ((bf16[512,2,128]{2,1,0:T(2,128)(2,1)}), bf16[512,2,128]{2,1,0:T(2,128)(2,1)S(1)}, u32[]{:S(2)}, u32[]{:S(2)}) async-start(bf16[512,2,128]{2,1,0:T(2,128)(2,1)} %copy.71), calls=%async_computation.1 | async-start | bytes 524288 | tf_op jit(solution)/shard_map/all_to_all | solution.py:98
  59.5 0.7 copy-start.2

commit v2 on v1

v2 whole, which is shorter than its diff:
```python
import functools
import math

import jax
import jax.numpy as jnp
import numpy as np
from jax import lax
from jax.experimental import pallas as pl
from jax.experimental.pallas import tpu as pltpu
from jax.sharding import PartitionSpec as P

CH = 64
MX = 32
MT = 16
MR = 16
BF = jnp.bfloat16
F32 = jnp.float32
VMEM_LIMIT = 48 * 1024 * 1024


def cosine_table(extent, wanted):
    places = np.arange(extent) + 0.5
    orders = np.arange(wanted)
    table = math.sqrt(2.0 / extent) * np.cos(math.pi * places[:, None] * orders[None, :] / extent)
    table[:, 0] *= 1.0 / math.sqrt(2.0)
    return table.astype(np.float32).astype(jnp.bfloat16).astype(np.float32)


def cycle_table(extent, half_modes):
    angles = 2.0 * math.pi * (np.arange(extent) + 0.5) / extent
    orders = np.arange(half_modes)
    cosines = math.sqrt(2.0 / extent) * np.cos(angles[:, None] * orders[None, :])
    cosines[:, 0] *= 1.0 / math.sqrt(2.0)
    sines = math.sqrt(2.0 / extent) * np.sin(angles[:, None] * (orders[None, :] + 1.0))
    table = np.concatenate([cosines, sines], axis=1)
    return table.astype(np.float32).astype(jnp.bfloat16).astype(np.float32)


def make_tables(axial, cycle, radial, cycle_devices):
    sector = cycle // cycle_devices
    pairs = 2 * MT * MR
    radial_table, axial_table = cosine_table(radial, MR), cosine_table(axial, MX)
    cycle_all = cycle_table(cycle, MT)
    tables = {}
    swap = np.zeros((16, 16, 16, 16), np.float32)
    for a in range(16):
        for b in range(16):
            swap[a, b, b, a] = 1.0
    tables["swap"] = swap.reshape(256, 256)
    ends = np.zeros((32, radial), np.float32)
    ends[:MR] = radial_table.T
    ends[MR:] = 1.0
    tables["ends"] = ends
    forward = np.zeros((cycle_devices, 2 * MT, MR, 2, sector, MR), np.float32)
    for k in range(MR):
        part = cycle_all.reshape(cycle_devices, sector, 2 * MT)
        forward[:, :, k, 0, :, k] = part.transpose(0, 2, 1)
    forward = forward.reshape(cycle_devices, 2 * pairs, sector * MR)
    tables["forward"] = forward
    tables["inverse"] = forward.transpose(0, 2, 1)
    rows = np.zeros((pairs, 2, 128), np.float32)
    for p in range(pairs):
        rows[p, 1, CH if p % 8 == 7 else p // 8] = 1.0
    tables["place"] = rows.reshape(2 * pairs, 128)
    pick = np.zeros((80, pairs, 2), np.float32)
    for i in range(CH):
        pick[i, 8 * i, 1] = 1.0
    pick[CH, 7, 1] = 1.0
    tables["pick"] = pick.reshape(80, 2 * pairs)
    gather = np.zeros((80, cycle_devices, pairs // cycle_devices, 2), np.float32)
    ax_devices = pairs // cycle_devices
    slab = axial // ax_devices
    by_slab = axial_table.reshape(ax_devices, slab, MX)
    gather[: slab * MX, :, :, 0] = by_slab.transpose(1, 2, 0).reshape(slab * MX, 1, ax_devices)
    gather[slab * MX :, :, :, 1] = 1.0
    tables["gather"] = gather.reshape(80, 2 * pairs)
    spread = np.zeros((ax_devices, 2, slab * MX), np.float32)
    spread[:, 0, :] = by_slab.reshape(ax_devices, slab * MX)
    tables["spread"] = spread.reshape(2 * ax_devices, slab * MX)
    halves = (np.arange(128)[:, None] // 64 == np.arange(128)[None, :] // 64).astype(np.float32)
    tables["halves"] = np.concatenate([halves, halves], axis=0)
    tables["radial"] = np.tile(radial_table.T, (sector, 1))
    tables["same"] = (np.arange(sector * MR)[None, :] // MR == np.arange(sector)[:, None]).astype(np.float32)
    return {name: value.astype(jnp.float32 if name == "same" else jnp.bfloat16) for name, value in tables.items()}


def gelu_slope(values):
    density = jnp.exp(-0.5 * values * values) * (1.0 / math.sqrt(2.0 * math.pi))
    return 0.5 * (1.0 + lax.erf(values * (1.0 / math.sqrt(2.0)))) + values * density


def dot_nn(a, b):
    return lax.dot_general(a, b, (((1,), (0,)), ((), ())), preferred_element_type=F32)


def dot_nt(a, b):
    return lax.dot_general(a, b, (((1,), (1,)), ((), ())), preferred_element_type=F32)


def split_halves(values):
    lane = lax.broadcasted_iota(jnp.int32, values.shape, 1)
    high = values.astype(BF).astype(F32)
    return jnp.where(lane < 64, high, pltpu.roll(values - high, 64, 1))


def first_kernel(steps, where, layer_ref, pre_ref, grad_ref, swap_ref, ends_ref, place_ref, forward_hbm,
                 slope_ref, sent_ref, layer_rows, grad_rows, coefs, forward, sem):
    step = pl.program_id(0)
    copy = pltpu.make_async_copy(forward_hbm.at[where[0]], forward, sem)

    @pl.when(step == 0)
    def _():
        copy.start()

    group = layer_ref.shape[0]
    slope = (grad_ref[...].astype(F32) * gelu_slope(pre_ref[...].astype(F32))).astype(BF)
    slope_ref[...] = slope
    layer = layer_ref[...]
    swap = swap_ref[...]
    for part in range(group // 16):
        for x in range(2):
            rows = pl.ds(pl.multiple_of(x * CH + step * group + part * 16, 16), 16)
            both = jnp.concatenate(
                [layer[part * 16 : part * 16 + 16, x].reshape(256, 128), slope[part * 16 : part * 16 + 16, x].reshape(256, 128)],
                axis=1,
            )
            moved = dot_nn(swap, both).astype(BF)
            layer_rows[:, rows, :] = moved[:, :128].reshape(16, 16, 128)
            grad_rows[:, rows, :] = moved[:, 128:].reshape(16, 16, 128)

    @pl.when(step == steps - 1)
    def _():
        point = jnp.zeros((128, 128), F32)
        bias = jnp.zeros((16, 128), F32)
        for t in range(16):
            left = jnp.concatenate([layer_rows[t], ends_ref[...]], axis=0)
            out = dot_nt(left, grad_rows[t])
            point += out[:128]
            coefs[t * MR : (t + 1) * MR, :] = out[128:144].astype(BF)
            bias += out[144:]
        point = point[:64] + pltpu.roll(point[64:], 64, 1)
        bias = bias + pltpu.roll(bias, 64, 1)
        sums = jnp.concatenate([split_halves(point), split_halves(bias), jnp.zeros((48, 128), F32)], axis=0)
        copy.wait()
        sent = dot_nn(forward[...], coefs[...]) + dot_nn(place_ref[...], sums.astype(BF))
        sent_ref[...] = sent.astype(BF)


def first(layer_input, pre_act, out_grad, tables):
    steps = 4
    group = CH // steps
    field = pl.BlockSpec((group, 2, 16, 128), lambda s, where: (s, 0, 0, 0))

    def whole(shape):
        return pl.BlockSpec(shape, lambda s, where: (0,) * len(shape))

    where = lax.axis_index("az").astype(jnp.int32).reshape(1)
    return pl.pallas_call(
        functools.partial(first_kernel, steps),
        grid_spec=pltpu.PrefetchScalarGridSpec(
            num_scalar_prefetch=1,
            grid=(steps,),
            in_specs=[
                field, field, field, whole((256, 256)), whole((32, 128)), whole((1024, 128)),
                pl.BlockSpec(memory_space=pl.ANY),
            ],
            out_specs=[field, whole((1024, 128))],
            scratch_shapes=[
                pltpu.VMEM((16, 128, 128), BF),
                pltpu.VMEM((16, 128, 128), BF),
                pltpu.VMEM((256, 128), BF),
                pltpu.VMEM((1024, 256), BF),
                pltpu.SemaphoreType.DMA,
            ],
        ),
        out_shape=[
            jax.ShapeDtypeStruct((CH, 2, 16, 128), BF),
            jax.ShapeDtypeStruct((1024, 128), BF),
        ],
        compiler_params=pltpu.CompilerParams(vmem_limit_bytes=60 * 1024 * 1024),
        name="slope_and_modes",
    )(where, layer_input, pre_act, out_grad, tables["swap"], tables["ends"], tables["place"], tables["forward"])


def middle_kernel(gain, norm, got_ref, gather_ref, weight_ref, halves_ref, spread_ref, mode_ref, sent_ref, stack):
    full = dot_nn(gather_ref[...], got_ref[...])
    lane = lax.broadcasted_iota(jnp.int32, (32, 128), 1)
    picked = jnp.where(lane < 64, full[:32], full[32:64])
    mode = (gain * (picked + pltpu.roll(picked, 64, 1))).astype(BF)
    mode_ref[...] = mode
    mode_wide = mode.astype(F32)
    for c in range(32):
        product = weight_ref[0, :, c * 128 : (c + 1) * 128].astype(F32) * mode_wide
        high = product.astype(BF)
        stack[c * 32 : (c + 1) * 32, :128] = high
        stack[c * 32 : (c + 1) * 32, 128:] = (product - high.astype(F32)).astype(BF)
    summed = dot_nn(stack[...], halves_ref[...])
    coef = jnp.zeros((32, 128), F32)
    for c in range(32):
        coef = jnp.where(lane % 64 == c, summed[c * 32 : (c + 1) * 32], coef)
    coef = jnp.concatenate([coef, pltpu.roll(coef, 32, 1)], axis=0).astype(BF)
    slabs = dot_nn(spread_ref[...], coef)
    sums = full[64:80]
    sums = split_halves((sums + pltpu.roll(sums, 64, 1)) * norm)
    row = lax.broadcasted_iota(jnp.int32, (128, 128), 0)
    slabs = jnp.where(row % 2 == 0, slabs, sums[:1]).astype(BF)
    for az in range(8):
        sent_ref[az] = slabs


def middle(got, spec_weight, tables, gain, norm):
    return pl.pallas_call(
        functools.partial(middle_kernel, gain, norm),
        out_shape=[jax.ShapeDtypeStruct((32, 128), BF), jax.ShapeDtypeStruct((8, 128, 128), BF)],
        scratch_shapes=[pltpu.VMEM((1024, 256), BF)],
        compiler_params=pltpu.CompilerParams(vmem_limit_bytes=VMEM_LIMIT),
        name="modes_and_mixing",
    )(got, tables["gather"], spec_weight, tables["halves"], tables["spread"])


def last_kernel(got_ref, pick_ref, radial_ref, same_ref, inverse_ref, point_ref,
                field_ref, weight_ref, bias_ref, columns, wide):
    step = pl.program_id(0)
    group = field_ref.shape[0]

    @pl.when(step == 0)
    def _():
        got = got_ref[...]
        columns[...] = jnp.transpose(dot_nn(inverse_ref[...], got))
        sums = dot_nn(pick_ref[...], got)
        sums = sums + pltpu.roll(sums, 64, 1)
        weight_ref[...] = sums[:64, :64]
        bias_ref[...] = sums[64:72]

    same = same_ref[...]
    for at in range(group):
        for x in range(2):
            place = (at % 2) * 64 + x * 32 + at // 2 + step * (group // 2)
            value = jnp.broadcast_to(columns[pl.ds(place, 1), :], (16, 256)) * same
            wide[(at * 2 + x) * 16 : (at * 2 + x) * 16 + 16, :] = value.astype(BF)
    spectral = dot_nn(wide[...], radial_ref[...])
    field_ref[...] = (spectral.reshape(group, 2, 16, 128) + point_ref[...]).astype(BF)


def last(got, inverse, point_part, tables):
    steps = 4
    group = CH // steps
    field = pl.BlockSpec((group, 2, 16, 128), lambda s: (s, 0, 0, 0))

    def whole(shape):
        return pl.BlockSpec(shape, lambda s: (0,) * len(shape))

    return pl.pallas_call(
        last_kernel,
        grid=(steps,),
        in_specs=[
            whole((1024, 128)), whole((80, 1024)), whole((256, 128)), whole((16, 256)), whole((256, 1024)), field,
        ],
        out_specs=[field, whole((64, 64)), whole((8, 128))],
        scratch_shapes=[pltpu.VMEM((128, 256), F32), pltpu.VMEM((group * 32, 256), BF)],
        out_shape=[
            jax.ShapeDtypeStruct((CH, 2, 16, 128), BF),
            jax.ShapeDtypeStruct((CH, CH), F32),
            jax.ShapeDtypeStruct((8, 128), F32),
        ],
        compiler_params=pltpu.CompilerParams(vmem_limit_bytes=VMEM_LIMIT),
        name="modes_to_field",
    )(got, tables["pick"], tables["radial"], tables["same"], inverse, point_part)


def exchange(rows, devices):
    sent = rows.reshape(devices, 2, 128)
    return lax.all_to_all(sent, ("az", "ax"), 0, 0, tiled=True).reshape(2 * devices, 128)


def per_device(layer_input, pre_act, out_grad, point_weight, spec_weight, saved_coeffs):
    axial_devices = lax.axis_size("ax")
    cycle_devices = lax.axis_size("az")
    devices = axial_devices * cycle_devices
    axial_total = layer_input.shape[1] * axial_devices
    cycle_total = layer_input.shape[2] * cycle_devices
    radial_length = layer_input.shape[3]
    cells_total = axial_total * cycle_total * radial_length
    gain = math.sqrt(cells_total / (2.0 * MX * MT * MR))
    norm = 1.0 / math.sqrt(cells_total)
    tables = make_tables(axial_total, cycle_total, radial_length, cycle_devices)

    grad_pre, sent = first(layer_input, pre_act, out_grad, tables)
    got = exchange(sent, devices)
    mode_grad, sent = middle(got, spec_weight, tables, gain, norm)
    got = exchange(sent.reshape(2 * devices, 128), devices)
    saved_modes = saved_coeffs.reshape(MX, CH).astype(F32)
    spec_grad = (
        (saved_modes[:, :, None] * mode_grad[:, :CH].astype(F32)[:, None, :]).astype(BF).reshape(1, MX, CH * CH)
    )
    inverse, _ = lax.optimization_barrier((tables["inverse"], mode_grad))
    inverse = lax.dynamic_index_in_dim(inverse, lax.axis_index("az"), 0, keepdims=False)
    point_part = jnp.einsum("io,oxtr->ixtr", point_weight, grad_pre, preferred_element_type=F32)
    input_grad, point_grad, bias_rows = last(got, inverse, point_part, tables)
    return (input_grad, point_grad, bias_rows[0, :CH], spec_grad)


def solution(mesh):
    return jax.shard_map(
        per_device,
        mesh=mesh,
        in_specs=(
            P(None, "ax", "az", None),
            P(None, "ax", "az", None),
            P(None, "ax", "az", None),
            P(),
            P(("az", "ax"), None, None),
            P(("az", "ax"), None),
        ),
        out_specs=(P(None, "ax", "az", None), P(), P(), P(("az", "ax"), None, None)),
        check_vma=False,
    )
```

time: 84.3 us -> 76.4 us (0.906)
  Pallas kernels: 0 us -> 9.73 us
  local copies, waits for them, and re-layouts: 11 us -> 3.5 us
  other arithmetic: 5.26 us -> 0.37 us
  matrix products: 4.83 us -> 1.34 us
  waiting for transfers between devices: 31.1 us -> 29.7 us
    pallas_call x0 -> x3, Pallas kernels: none -> 9.73 us  [the longest x1 5.77 us: first(): pl.pallas_call(functools.partial(first_kernel, steps), grid_spec=pltpu.Pr...]
    dot_general x8 -> x0, matrix products: 4.53 us -> none  [the longest x1 1.7 us: per_device(): jnp.einsum('ixtk,rk->ixtr', radial_modes, radial_table, preferred_element...]
    reduce_sum x3 -> x0, other arithmetic: 2.64 us -> none  [the longest x1 2.03 us: per_device(): bias_local = jnp.sum(grad_pre.astype(jnp.float32), axis=(1, 2, 3))]
    slice x4 -> x0, local copies, waits for them, and re-layouts: 2.62 us -> none  [the longest x1 0.75 us: per_device(): cycle_modes = got[:, 0].reshape(2 * MT, MR, slab_length, CH)]
    another operation x7 -> x0, local copies, waits for them, and re-layouts: 2.41 us -> none  [the longest x3 1.15 us: per_device(): sent = jnp.stack([modes, sums_row], axis=1)]
    add x1 -> x0, other arithmetic: 1.84 us -> none  [per_device(): got[:, 1, :share].astype(jnp.float32)]
    convert_element_type x6 -> x2, local copies, waits for them, and re-layouts: 3.07 us -> 1.24 us  [the longest x1 1.17 us: per_device(): (saved_modes[:, :, None] * mode_grad[:, :CH].astype(F32)[:, None, :]).ast...]
    squeeze x0 -> x2, local copies, waits for them, and re-layouts: none -> 1.59 us  [the longest x1 1.08 us: per_device(): lax.dynamic_index_in_dim(inverse, lax.axis_index('az'), 0, keepdims=False)]
  transfers between devices with their start and end apart: 2 -> 2, of which waited for: 2 -> 2; matrix products, arithmetic and copies ran while one was open for 3% -> 6% of each run, Pallas kernels for 0% -> 0%
where the time goes in v2:
time: 76.4 us; the launch traced here: 76 us
  starting transfers between devices  30.5 us (40%)
  waiting for transfers between devices  29.7 us (39%)
  Pallas kernels  9.73 us (13%)
  local copies, waits for them, and re-layouts  3.5 us (5%)
  matrix products  1.34 us (2%)
  between operations  0.8 us (1%)
    all_to_all x2, starting transfers between devices, exchange(): lax.all_to_all(sent, ('az', 'ax'), 0, 0, tiled=True)  30.5 us
    all_to_all x2, waiting for transfers between devices, exchange(): lax.all_to_all(sent, ('az', 'ax'), 0, 0, tiled=True)  29.7 us
    pallas_call x1, Pallas kernels, first(): pl.pallas_call(functools.partial(first_kernel, steps), grid_spec=pltpu.Pr...  5.77 us
    pallas_call x1, Pallas kernels, last(): pl.pallas_call(last_kernel, grid=(steps,), in_specs=[whole((1024, 128)),...  2.49 us
  transfers between devices with their start and end apart: 2, of which 2 were waited for; matrix products, arithmetic and copies ran while one was open for 6% of the time, Pallas kernels for 0%

profile of v2, /device:TPU:1, one launch (start us, length us, event | category | flops | bytes accessed | tf_op | source)
XLA Modules:
  0.0 76.0 jit_solution(17566249503502092081)
XLA Ops:
  0.6 0.0 copy-start
  0.7 0.0 copy-start.8
  0.7 0.0 copy-start.1
  0.7 0.0 copy-start.3
  0.7 0.0 copy-start.5
  0.7 0.0 copy-start.6
  0.7 5.8 %slope_and_modes.1 = (bf16[64,2,16,128]{3,2,1,0:T(8,128)(2,1)}, bf16[1024,128]{1,0:T(8,128)(2,1)}) custom-call(s32[1]{0:T(128)} %bitcast.where, bf16[64,2,16,128]{3,2,1,0:T(8,128)(2,1)} %layer_ref.1, bf16[64,2,16,128]{3,2,1,0:T(8,128)(2,1)} %pre_ref.1, bf16[64,2,16,128]{3,2,1,0:T(8,128)(2,1)} %grad_ref.1, bf16[256,256]{1,0:T(8,128)(2,1)} %constant.32.clone.swap_ref, ...), custom_call_target="tpu_custom_call" | custom-call | tf_op jit(solution)/shard_map/slope_and_modes/pallas_call | solution.py:158
  6.5 0.0 copy-start.2
  6.5 0.0 copy-start.4
  6.5 0.0 copy-start.7
  6.5 22.2 %all-to-all-start = ((bf16[512,2,128]{2,1,0:T(2,128)(2,1)}), bf16[512,2,128]{2,1,0:T(2,128)(2,1)S(1)}, u32[]{:S(2)}, u32[]{:S(2)}) async-start(bf16[512,2,128]{2,1,0:T(2,128)(2,1)} %bitcast.20), calls=%async_computation | async-start | bytes 524288 | tf_op jit(solution)/shard_map/all_to_all | solution.py:273
  28.7 0.0 copy-done
  28.7 1.3 %fusion = f32[2,16,128,64]{2,3,1,0:T(8,128)S(1)} fusion(bf16[64,2,16,128]{3,2,1,0:T(8,128)(2,1)} %get-tuple-element.16, bf16[64,64]{1,0:T(8,128)(2,1)S(1)} %copy-done), kind=kOutput, calls=%fused_computation.2 | convolution fusion | flops 33554432 | bytes 1581056 | tf_op jit(solution)/shard_map/io,oxtr->ixtr/dot_general | solution.py:298
  30.1 0.6 copy.27
  30.7 0.0 copy-done.8
  30.7 0.1 reshape.60
  30.8 15.2 %all-to-all-done = bf16[512,2,128]{2,1,0:T(2,128)(2,1)S(1)} async-done(((bf16[512,2,128]{2,1,0:T(2,128)(2,1)}), bf16[512,2,128]{2,1,0:T(2,128)(2,1)S(1)}, u32[]{:S(2)}, u32[]{:S(2)}) %all-to-all-start) | async-done | bytes 262176 | tf_op jit(solution)/shard_map/all_to_all | solution.py:273
  46.0 0.0 copy-done.1
  46.0 0.0 copy-done.3
  46.0 0.0 copy-done.5
  46.0 0.0 copy-done.6
  46.0 1.5 %modes_and_mixing.1 = (bf16[32,128]{1,0:T(8,128)(2,1)S(1)}, bf16[8,128,128]{2,1,0:T(8,128)(2,1)}) custom-call(bf16[1024,128]{1,0:T(8,128)(2,1)S(1)} %bitcast.18, bf16[80,1024]{1,0:T(8,128)(2,1)S(1)} %copy-done.3, bf16[1,32,4096]{2,1,0:T(8,128)(2,1)S(1)} %copy-done.1, bf16[256,128]{1,0:T(8,128)(2,1)S(1)} %copy-done.5, bf16[128,64]{1,0:T(8,128)(2,1)S(1)} %copy-done.6), custom_call_target="tpu_custom_call" | custom-call | tf_op jit(solution)/shard_map/modes_and_mixing/pallas_call | solution.py:212
  47.5 8.3 %all-to-all-start.1 = ((bf16[512,2,128]{2,1,0:T(2,128)(2,1)}), bf16[512,2,128]{2,1,0:T(2,128)(2,1)S(1)}, u32[]{:S(2)}, u32[]{:S(2)}) async-start(bf16[512,2,128]{2,1,0:T(2,128)(2,1)} %bitcast.3), calls=%async_computation.1 | async-start | bytes 524288 | tf_op jit(solution)/shard_map/all_to_all | solution.py:273
  55.8 0.3 multiply_convert_fusion
  56.2 1.2 %convert_element_type.30 = bf16[1,32,4096]{2,1,0:T(8,128)(2,1)} reshape(bf16[32,64,64]{2,1,0:T(8,128)(2,1)S(1)} %multiply_convert_fusion) | data formatting | bytes 524288 | tf_op jit(solution)/shard_map/convert_element_type | solution.py:294
  57.3 1.1 %dynamic-slice_bitcast_fusion.inverse_ref = bf16[256,1024]{1,0:T(8,128)(2,1)S(1)} fusion(bf16[8,256,1024]{2,1,0:T(8,128)(2,1)} %constant.39.clone, s32[]{:T(128)S(6)} %select_n.4), kind=kLoop, calls=%fused_computation.4 | loop fusion | bytes 1048580 | tf_op jit(solution)/shard_map/jit(dynamic_index_in_dim)/squeeze | solution.py:297
  58.4 14.6 %all-to-all-done.1 = bf16[512,2,128]{2,1,0:T(2,128)(2,1)S(1)} async-done(((bf16[512,2,128]{2,1,0:T(2,128)(2,1)}), bf16[512,2,128]{2,1,0:T(2,128)(2,1)S(1)}, u32[]{:S(2)}, u32[]{:S(2)}) %all-to-all-start.1) | async-done | bytes 262176 | tf_op jit(solution)/shard_map/all_to_all | solution.py:273
  73.0 0.0 copy-done.2
  73.0 0.0 copy-done.4
  73.0 0.0 copy-done.7
  73.0 2.5 %modes_to_field.1 = (bf16[64,2,16,128]{3,2,1,0:T(8,128)(2,1)}, f32[64,64]{1,0:T(8,128)}, f32[8,128]{1,0:T(8,128)S(1)}) custom-call(bf16[1024,128]{1,0:T(8,128)(2,1)S(1)} %bitcast.19, bf16[80,1024]{1,0:T(8,128)(2,1)S(1)} %copy-done.2, bf16[256,128]{1,0:T(8,128)(2,1)S(1)} %copy-done.4, f32[16,256]{1,0:T(8,128)S(1)} %copy-done.7, ...), custom_call_target="tpu_custom_call" | custom-call | tf_op jit(solution)/shard_map/modes_to_field/pallas_call | solution.py:253
  75.5 0.5 slice_bitcast_fusion
  (2 shorter events, 0.0 us)
Async XLA Ops:
  0.6 28.1 %copy-start = (bf16[64,64]{1,0:T(8,128)(2,1)S(1)}, bf16[64,64]{1,0:T(8,128)(2,1)}, u32[]{:S(2)}) copy-start(bf16[64,64]{1,0:T(8,128)(2,1)} %param.20) | copy-start | bytes 24580
  0.7 30.0 %copy-start.8 = (bf16[1,2048]{1,0:T(2,128)(2,1)S(1)}, bf16[1,2048]{1,0:T(2,128)(2,1)}, u32[]{:S(2)}) copy-start(bf16[1,2048]{1,0:T(2,128)(2,1)} %param.22) | copy-start | bytes 12292
  0.7 45.3 %copy-start.1 = (bf16[1,32,4096]{2,1,0:T(8,128)(2,1)S(1)}, bf16[1,32,4096]{2,1,0:T(8,128)(2,1)}, u32[]{:S(2)}) copy-start(bf16[1,32,4096]{2,1,0:T(8,128)(2,1)} %weight_ref.1) | copy-start | bytes 786436
  0.7 45.3 %copy-start.3 = (bf16[80,1024]{1,0:T(8,128)(2,1)S(1)}, bf16[80,1024]{1,0:T(8,128)(2,1)}, u32[]{:S(2)}) copy-start(bf16[80,1024]{1,0:T(8,128)(2,1)} %constant.36.clone.gather_ref) | copy-start | bytes 491524
  0.7 45.3 %copy-start.5 = (bf16[256,128]{1,0:T(8,128)(2,1)S(1)}, bf16[256,128]{1,0:T(8,128)(2,1)}, u32[]{:S(2)}) copy-start(bf16[256,128]{1,0:T(8,128)(2,1)} %constant.37.clone.halves_ref) | copy-start | bytes 196612
  0.7 45.3 %copy-start.6 = (bf16[128,64]{1,0:T(8,128)(2,1)S(1)}, bf16[128,64]{1,0:T(8,128)(2,1)}, u32[]{:S(2)}) copy-start(bf16[128,64]{1,0:T(8,128)(2,1)} %constant.38.clone.spread_ref) | copy-start | bytes 49156
  6.5 66.5 %copy-start.2 = (bf16[80,1024]{1,0:T(8,128)(2,1)S(1)}, bf16[80,1024]{1,0:T(8,128)(2,1)}, u32[]{:S(2)}) copy-start(bf16[80,1024]{1,0:T(8,128)(2,1)} %constant.40.clone.pick_ref) | copy-start | bytes 491524
  6.5 66.5 %copy-start.4 = (bf16[256,128]{1,0:T(8,128)(2,1)S(1)}, bf16[256,128]{1,0:T(8,128)(2,1)}, u32[]{:S(2)}) copy-start(bf16[256,128]{1,0:T(8,128)(2,1)} %constant.41.clone.radial_ref) | copy-start | bytes 196612
  6.5 66.5 %copy-start.7 = (f32[16,256]{1,0:T(8,128)S(1)}, f32[16,256]{1,0:T(8,128)}, u32[]{:S(2)}) copy-start(f32[16,256]{1,0:T(8,128)} %constant.42.clone.same_ref) | copy-start | bytes 49156
  6.5 39.4 %all-to-all-start = ((bf16[512,2,128]{2,1,0:T(2,128)(2,1)}), bf16[512,2,128]{2,1,0:T(2,128)(2,1)S(1)}, u32[]{:S(2)}, u32[]{:S(2)}) async-start(bf16[512,2,128]{2,1,0:T(2,128)(2,1)} %bitcast.20), calls=%async_computation | async-start | bytes 524288 | tf_op jit(solution)/shard_map/all_to_all | solution.py:273
  47.5 25.5 %all-to-all-start.1 = ((bf16[512,2,128]{2,1,0:T(2,128)(2,1)}), bf16[512,2,128]{2,1,0:T(2,128)(2,1)S(1)}, u32[]{:S(2)}, u32[]{:S(2)}) async-start(bf16[512,2,128]{2,1,0:T(2,128)(2,1)} %bitcast.3), calls=%async_computation.1 | async-start | bytes 524288 | tf_op jit(solution)/shard_map/all_to_all | solution.py:273

commit v3 on v2

--- a/solution.py
+++ b/solution.py
@@ -103,83 +103,88 @@
     return jnp.where(lane < 64, high, pltpu.roll(values - high, 64, 1))
 
 
-def first_kernel(steps, where, layer_ref, pre_ref, grad_ref, swap_ref, ends_ref, place_ref, forward_hbm,
-                 slope_ref, sent_ref, layer_rows, grad_rows, coefs, forward, sem):
-    step = pl.program_id(0)
-    copy = pltpu.make_async_copy(forward_hbm.at[where[0]], forward, sem)
-
-    @pl.when(step == 0)
-    def _():
+def first_kernel(where, swap_ref, ends_ref, layer_hbm, pre_hbm, grad_hbm, place_hbm, forward_hbm,
+                 slope_hbm, sent_ref, layer, pre, grad, slope, layer_rows, grad_rows, coefs, place, forward,
+                 in_sem, out_sem, table_sem):
+    chunks = in_sem.shape[0]
+    group = CH // chunks
+    copies = []
+    for c in range(chunks):
+        part = pl.ds(c * group, group)
+        pairs = ((pre_hbm, pre), (grad_hbm, grad), (layer_hbm, layer))
+        copies.append([pltpu.make_async_copy(a.at[part], b.at[part], in_sem.at[c, n]) for n, (a, b) in enumerate(pairs)])
+        for copy in copies[-1]:
+            copy.start()
+    tables = [
+        pltpu.make_async_copy(forward_hbm.at[where[0]], forward, table_sem.at[0]),
+        pltpu.make_async_copy(place_hbm, place, table_sem.at[1]),
+    ]
+    for copy in tables:
         copy.start()
-
-    group = layer_ref.shape[0]
-    slope = (grad_ref[...].astype(F32) * gelu_slope(pre_ref[...].astype(F32))).astype(BF)
-    slope_ref[...] = slope
-    layer = layer_ref[...]
     swap = swap_ref[...]
-    for part in range(group // 16):
-        for x in range(2):
-            rows = pl.ds(pl.multiple_of(x * CH + step * group + part * 16, 16), 16)
-            both = jnp.concatenate(
-                [layer[part * 16 : part * 16 + 16, x].reshape(256, 128), slope[part * 16 : part * 16 + 16, x].reshape(256, 128)],
-                axis=1,
-            )
-            moved = dot_nn(swap, both).astype(BF)
-            layer_rows[:, rows, :] = moved[:, :128].reshape(16, 16, 128)
-            grad_rows[:, rows, :] = moved[:, 128:].reshape(16, 16, 128)
-
-    @pl.when(step == steps - 1)
-    def _():
-        point = jnp.zeros((128, 128), F32)
-        bias = jnp.zeros((16, 128), F32)
-        for t in range(16):
-            left = jnp.concatenate([layer_rows[t], ends_ref[...]], axis=0)
-            out = dot_nt(left, grad_rows[t])
-            point += out[:128]
-            coefs[t * MR : (t + 1) * MR, :] = out[128:144].astype(BF)
-            bias += out[144:]
-        point = point[:64] + pltpu.roll(point[64:], 64, 1)
-        bias = bias + pltpu.roll(bias, 64, 1)
-        sums = jnp.concatenate([split_halves(point), split_halves(bias), jnp.zeros((48, 128), F32)], axis=0)
+    leaving = []
+    for c in range(chunks):
+        part = pl.ds(c * group, group)
+        for copy in copies[c]:
+            copy.wait()
+        slope[part] = (grad[part].astype(F32) * gelu_slope(pre[part].astype(F32))).astype(BF)
+        leaving.append(pltpu.make_async_copy(slope.at[part], slope_hbm.at[part], out_sem.at[c]))
+        leaving[-1].start()
+        for at in range(c * group, (c + 1) * group, 16):
+            for x in range(2):
+                both = jnp.concatenate(
+                    [layer[at : at + 16, x].reshape(256, 128), slope[at : at + 16, x].reshape(256, 128)], axis=1
+                )
+                moved = dot_nn(swap, both).astype(BF)
+                rows = slice(x * CH + at, x * CH + at + 16)
+                layer_rows[:, rows, :] = moved[:, :128].reshape(16, 16, 128)
+                grad_rows[:, rows, :] = moved[:, 128:].reshape(16, 16, 128)
+    point = jnp.zeros((128, 128), F32)
+    bias = jnp.zeros((16, 128), F32)
+    for t in range(16):
+        left = jnp.concatenate([layer_rows[t], ends_ref[...]], axis=0)
+        out = dot_nt(left, grad_rows[t])
+        point += out[:128]
+        coefs[t * MR : (t + 1) * MR, :] = out[128:144].astype(BF)
+        bias += out[144:]
+    point = point[:64] + pltpu.roll(point[64:], 64, 1)
+    bias = bias + pltpu.roll(bias, 64, 1)
+    sums = jnp.concatenate([split_halves(point), split_halves(bias), jnp.zeros((48, 128), F32)], axis=0)
+    for copy in tables:
         copy.wait()
-        sent = dot_nn(forward[...], coefs[...]) + dot_nn(place_ref[...], sums.astype(BF))
-        sent_ref[...] = sent.astype(BF)
+    sent = dot_nn(forward[...], coefs[...]) + dot_nn(place[...], sums.astype(BF))
+    sent_ref[...] = sent.astype(BF)
+    for copy in leaving:
+        copy.wait()
 
 
 def first(layer_input, pre_act, out_grad, tables):
-    steps = 4
-    group = CH // steps
-    field = pl.BlockSpec((group, 2, 16, 128), lambda s, where: (s, 0, 0, 0))
-
-    def whole(shape):
-        return pl.BlockSpec(shape, lambda s, where: (0,) * len(shape))
-
+    chunks = 2
+    shape = (CH, 2, 16, 128)
     where = lax.axis_index("az").astype(jnp.int32).reshape(1)
+    hbm, vmem = pl.BlockSpec(memory_space=pl.ANY), pl.BlockSpec(memory_space=pltpu.VMEM)
     return pl.pallas_call(
-        functools.partial(first_kernel, steps),
-        grid_spec=pltpu.PrefetchScalarGridSpec(
-            num_scalar_prefetch=1,
-            grid=(steps,),
-            in_specs=[
-                field, field, field, whole((256, 256)), whole((32, 128)), whole((1024, 128)),
-                pl.BlockSpec(memory_space=pl.ANY),
-            ],
-            out_specs=[field, whole((1024, 128))],
-            scratch_shapes=[
-                pltpu.VMEM((16, 128, 128), BF),
-                pltpu.VMEM((16, 128, 128), BF),
-                pltpu.VMEM((256, 128), BF),
-                pltpu.VMEM((1024, 256), BF),
-                pltpu.SemaphoreType.DMA,
-            ],
-        ),
-        out_shape=[
-            jax.ShapeDtypeStruct((CH, 2, 16, 128), BF),
-            jax.ShapeDtypeStruct((1024, 128), BF),
+        first_kernel,
+        in_specs=[pl.BlockSpec(memory_space=pltpu.SMEM), vmem, vmem, hbm, hbm, hbm, hbm, hbm],
+        out_specs=[hbm, vmem],
+        scratch_shapes=[
+            pltpu.VMEM(shape, BF),
+            pltpu.VMEM(shape, BF),
+            pltpu.VMEM(shape, BF),
+            pltpu.VMEM(shape, BF),
+            pltpu.VMEM((16, 128, 128), BF),
+            pltpu.VMEM((16, 128, 128), BF),
+            pltpu.VMEM((256, 128), BF),
+            pltpu.VMEM((1024, 128), BF),
+            pltpu.VMEM((1024, 256), BF),
+            pltpu.SemaphoreType.DMA((chunks, 3)),
+            pltpu.SemaphoreType.DMA((chunks,)),
+            pltpu.SemaphoreType.DMA((2,)),
         ],
+        out_shape=[jax.ShapeDtypeStruct(shape, BF), jax.ShapeDtypeStruct((1024, 128), BF)],
         compiler_params=pltpu.CompilerParams(vmem_limit_bytes=60 * 1024 * 1024),
         name="slope_and_modes",
-    )(where, layer_input, pre_act, out_grad, tables["swap"], tables["ends"], tables["place"], tables["forward"])
+    )(where, tables["swap"], tables["ends"], layer_input, pre_act, out_grad, tables["place"], tables["forward"])
 
 
 def middle_kernel(gain, norm, got_ref, gather_ref, weight_ref, halves_ref, spread_ref, mode_ref, sent_ref, stack):
@@ -219,51 +224,54 @@
 
 
 def last_kernel(got_ref, pick_ref, radial_ref, same_ref, inverse_ref, point_ref,
-                field_ref, weight_ref, bias_ref, columns, wide):
-    step = pl.program_id(0)
-    group = field_ref.shape[0]
-
-    @pl.when(step == 0)
-    def _():
-        got = got_ref[...]
-        columns[...] = jnp.transpose(dot_nn(inverse_ref[...], got))
-        sums = dot_nn(pick_ref[...], got)
-        sums = sums + pltpu.roll(sums, 64, 1)
-        weight_ref[...] = sums[:64, :64]
-        bias_ref[...] = sums[64:72]
-
+                field_hbm, weight_ref, bias_ref, columns, wide, field, out_sem):
+    got = got_ref[...]
+    columns[...] = jnp.transpose(dot_nn(inverse_ref[...], got))
     same = same_ref[...]
-    for at in range(group):
-        for x in range(2):
-            place = (at % 2) * 64 + x * 32 + at // 2 + step * (group // 2)
-            value = jnp.broadcast_to(columns[pl.ds(place, 1), :], (16, 256)) * same
-            wide[(at * 2 + x) * 16 : (at * 2 + x) * 16 + 16, :] = value.astype(BF)
-    spectral = dot_nn(wide[...], radial_ref[...])
-    field_ref[...] = (spectral.reshape(group, 2, 16, 128) + point_ref[...]).astype(BF)
+    radial = radial_ref[...]
+    chunks = out_sem.shape[0]
+    group = CH // chunks
+    leaving = []
+    for c in range(chunks):
+        for at in range(group):
+            for x in range(2):
+                i = c * group + at
+                place = (i % 2) * 64 + x * 32 + i // 2
+                value = jnp.broadcast_to(columns[place : place + 1, :], (16, 256)) * same
+                wide[c, (at * 2 + x) * 16 : (at * 2 + x) * 16 + 16, :] = value.astype(BF)
+        part = slice(c * group, (c + 1) * group)
+        spectral = dot_nn(wide[c], radial)
+        field[part] = (spectral.reshape(group, 2, 16, 128) + point_ref[part]).astype(BF)
+        leaving.append(pltpu.make_async_copy(field.at[part], field_hbm.at[part], out_sem.at[c]))
+        leaving[-1].start()
+    sums = dot_nn(pick_ref[...], got)
+    sums = sums + pltpu.roll(sums, 64, 1)
+    weight_ref[...] = sums[:64, :64]
+    bias_ref[...] = sums[64, :64]
+    for copy in leaving:
+        copy.wait()
 
 
 def last(got, inverse, point_part, tables):
-    steps = 4
-    group = CH // steps
-    field = pl.BlockSpec((group, 2, 16, 128), lambda s: (s, 0, 0, 0))
-
-    def whole(shape):
-        return pl.BlockSpec(shape, lambda s: (0,) * len(shape))
-
+    chunks = 4
+    shape = (CH, 2, 16, 128)
+    hbm, vmem = pl.BlockSpec(memory_space=pl.ANY), pl.BlockSpec(memory_space=pltpu.VMEM)
     return pl.pallas_call(
         last_kernel,
-        grid=(steps,),
-        in_specs=[
-            whole((1024, 128)), whole((80, 1024)), whole((256, 128)), whole((16, 256)), whole((256, 1024)), field,
+        in_specs=[vmem] * 6,
+        out_specs=[hbm, vmem, vmem],
+        scratch_shapes=[
+            pltpu.VMEM((128, 256), F32),
+            pltpu.VMEM((chunks, CH // chunks * 32, 256), BF),
+            pltpu.VMEM(shape, BF),
+            pltpu.SemaphoreType.DMA((chunks,)),
         ],
-        out_specs=[field, whole((64, 64)), whole((8, 128))],
-        scratch_shapes=[pltpu.VMEM((128, 256), F32), pltpu.VMEM((group * 32, 256), BF)],
         out_shape=[
-            jax.ShapeDtypeStruct((CH, 2, 16, 128), BF),
+            jax.ShapeDtypeStruct(shape, BF),
             jax.ShapeDtypeStruct((CH, CH), F32),
-            jax.ShapeDtypeStruct((8, 128), F32),
+            jax.ShapeDtypeStruct((CH,), F32),
         ],
-        compiler_params=pltpu.CompilerParams(vmem_limit_bytes=VMEM_LIMIT),
+        compiler_params=pltpu.CompilerParams(vmem_limit_bytes=32 * 1024 * 1024),
         name="modes_to_field",
     )(got, tables["pick"], tables["radial"], tables["same"], inverse, point_part)
 
@@ -296,8 +304,8 @@
     inverse, _ = lax.optimization_barrier((tables["inverse"], mode_grad))
     inverse = lax.dynamic_index_in_dim(inverse, lax.axis_index("az"), 0, keepdims=False)
     point_part = jnp.einsum("io,oxtr->ixtr", point_weight, grad_pre, preferred_element_type=F32)
-    input_grad, point_grad, bias_rows = last(got, inverse, point_part, tables)
-    return (input_grad, point_grad, bias_rows[0, :CH], spec_grad)
+    input_grad, point_grad, bias_grad = last(got, inverse, point_part, tables)
+    return (input_grad, point_grad, bias_grad, spec_grad)
 
 
 def solution(mesh):

time: 76.4 us -> 74.9 us (0.980)
  Pallas kernels: 9.73 us -> 8.8 us
    pallas_call x2, Pallas kernels: 8.26 us -> 7.33 us  [the longest x1 5.23 us: first(): pl.pallas_call(first_kernel, in_specs=[pl.BlockSpec(memory_space=pltpu.SM...]
where the time goes in v3:
time: 74.9 us; the launch traced here: 74.6 us
  starting transfers between devices  30.5 us (41%)
  waiting for transfers between devices  29.7 us (40%)
  Pallas kernels  8.8 us (12%)
  local copies, waits for them, and re-layouts  2.99 us (4%)
  matrix products  1.35 us (2%)
  between operations  0.8 us (1%)
    all_to_all x2, starting transfers between devices, exchange(): lax.all_to_all(sent, ('az', 'ax'), 0, 0, tiled=True)  30.5 us
    all_to_all x2, waiting for transfers between devices, exchange(): lax.all_to_all(sent, ('az', 'ax'), 0, 0, tiled=True)  29.7 us
    pallas_call x1, Pallas kernels, first(): pl.pallas_call(first_kernel, in_specs=[pl.BlockSpec(memory_space=pltpu.SM...  5.23 us
    pallas_call x1, Pallas kernels, last(): pl.pallas_call(last_kernel, in_specs=[vmem] * 6, out_specs=[hbm, vmem, vm...  2.1 us
  transfers between devices with their start and end apart: 2, of which 2 were waited for; matrix products, arithmetic and copies ran while one was open for 6% of the time, Pallas kernels for 0%

profile of v3, /device:TPU:1, one launch (start us, length us, event | category | flops | bytes accessed | tf_op | source)
XLA Modules:
  0.0 74.6 jit_solution(9102167939652583321)
XLA Ops:
  0.6 0.0 copy-start
  0.7 0.0 copy-start.8
  0.7 0.0 copy-start.1
  0.7 0.0 copy-start.3
  0.7 0.0 copy-start.5
  0.7 0.0 copy-start.6
  0.7 5.2 %slope_and_modes.1 = (bf16[64,2,16,128]{3,2,1,0:T(8,128)(2,1)}, bf16[1024,128]{1,0:T(8,128)(2,1)}) custom-call(s32[1]{0:T(128)} %bitcast.where, bf16[256,256]{1,0:T(8,128)(2,1)} %constant.32.clone.swap_ref, bf16[32,128]{1,0:T(8,128)(2,1)} %constant.33.clone.ends_ref, bf16[64,2,16,128]{3,2,1,0:T(8,128)(2,1)} %layer_hbm.1, bf16[64,2,16,128]{3,2,1,0:T(8,128)(2,1)} %pre_hbm.1, ...), custom_call_target="tpu_custom_call" | custom-call | tf_op jit(solution)/shard_map/slope_and_modes/pallas_call | solution.py:166
  5.9 0.0 copy-start.2
  6.0 0.0 copy-start.4
  6.0 0.0 copy-start.7
  6.0 22.2 %all-to-all-start = ((bf16[512,2,128]{2,1,0:T(2,128)(2,1)}), bf16[512,2,128]{2,1,0:T(2,128)(2,1)S(1)}, u32[]{:S(2)}, u32[]{:S(2)}) async-start(bf16[512,2,128]{2,1,0:T(2,128)(2,1)} %bitcast.18), calls=%async_computation | async-start | bytes 524288 | tf_op jit(solution)/shard_map/all_to_all | solution.py:281
  28.2 0.0 copy-done
  28.2 1.4 %fusion = f32[2,16,128,64]{2,3,1,0:T(8,128)S(1)} fusion(bf16[64,2,16,128]{3,2,1,0:T(8,128)(2,1)} %get-tuple-element.16, bf16[64,64]{1,0:T(8,128)(2,1)S(1)} %copy-done), kind=kOutput, calls=%fused_computation.2 | convolution fusion | flops 33554432 | bytes 1581056 | tf_op jit(solution)/shard_map/io,oxtr->ixtr/dot_general | solution.py:306
  29.5 0.6 copy.27
  30.1 0.0 copy-done.8
  30.2 0.1 reshape.60
  30.3 15.2 %all-to-all-done = bf16[512,2,128]{2,1,0:T(2,128)(2,1)S(1)} async-done(((bf16[512,2,128]{2,1,0:T(2,128)(2,1)}), bf16[512,2,128]{2,1,0:T(2,128)(2,1)S(1)}, u32[]{:S(2)}, u32[]{:S(2)}) %all-to-all-start) | async-done | bytes 262176 | tf_op jit(solution)/shard_map/all_to_all | solution.py:281
  45.4 0.0 copy-done.1
  45.4 0.0 copy-done.3
  45.4 0.0 copy-done.5
  45.4 0.0 copy-done.6
  45.4 1.5 %modes_and_mixing.1 = (bf16[32,128]{1,0:T(8,128)(2,1)S(1)}, bf16[8,128,128]{2,1,0:T(8,128)(2,1)}) custom-call(bf16[1024,128]{1,0:T(8,128)(2,1)S(1)} %bitcast.16, bf16[80,1024]{1,0:T(8,128)(2,1)S(1)} %copy-done.3, bf16[1,32,4096]{2,1,0:T(8,128)(2,1)S(1)} %copy-done.1, bf16[256,128]{1,0:T(8,128)(2,1)S(1)} %copy-done.5, bf16[128,64]{1,0:T(8,128)(2,1)S(1)} %copy-done.6), custom_call_target="tpu_custom_call" | custom-call | tf_op jit(solution)/shard_map/modes_and_mixing/pallas_call | solution.py:217
  46.9 8.3 %all-to-all-start.1 = ((bf16[512,2,128]{2,1,0:T(2,128)(2,1)}), bf16[512,2,128]{2,1,0:T(2,128)(2,1)S(1)}, u32[]{:S(2)}, u32[]{:S(2)}) async-start(bf16[512,2,128]{2,1,0:T(2,128)(2,1)} %bitcast.3), calls=%async_computation.1 | async-start | bytes 524288 | tf_op jit(solution)/shard_map/all_to_all | solution.py:281
  55.3 0.3 multiply_convert_fusion
  55.6 1.2 %convert_element_type.30 = bf16[1,32,4096]{2,1,0:T(8,128)(2,1)} reshape(bf16[32,64,64]{2,1,0:T(8,128)(2,1)S(1)} %multiply_convert_fusion) | data formatting | bytes 524288 | tf_op jit(solution)/shard_map/convert_element_type | solution.py:302
  56.8 1.1 %dynamic-slice_bitcast_fusion.inverse_ref = bf16[256,1024]{1,0:T(8,128)(2,1)S(1)} fusion(bf16[8,256,1024]{2,1,0:T(8,128)(2,1)} %constant.39.clone, s32[]{:T(128)S(6)} %select_n.4), kind=kLoop, calls=%fused_computation.4 | loop fusion | bytes 1048580 | tf_op jit(solution)/shard_map/jit(dynamic_index_in_dim)/squeeze | solution.py:305
  57.9 14.6 %all-to-all-done.1 = bf16[512,2,128]{2,1,0:T(2,128)(2,1)S(1)} async-done(((bf16[512,2,128]{2,1,0:T(2,128)(2,1)}), bf16[512,2,128]{2,1,0:T(2,128)(2,1)S(1)}, u32[]{:S(2)}, u32[]{:S(2)}) %all-to-all-start.1) | async-done | bytes 262176 | tf_op jit(solution)/shard_map/all_to_all | solution.py:281
  72.4 0.0 copy-done.2
  72.5 0.0 copy-done.4
  72.5 0.0 copy-done.7
  72.5 2.1 %modes_to_field.1 = (bf16[64,2,16,128]{3,2,1,0:T(8,128)(2,1)}, f32[64,64]{1,0:T(8,128)}, f32[64]{0:T(128)}) custom-call(bf16[1024,128]{1,0:T(8,128)(2,1)S(1)} %bitcast.17, bf16[80,1024]{1,0:T(8,128)(2,1)S(1)} %copy-done.2, bf16[256,128]{1,0:T(8,128)(2,1)S(1)} %copy-done.4, f32[16,256]{1,0:T(8,128)S(1)} %copy-done.7, ...), custom_call_target="tpu_custom_call" | custom-call | tf_op jit(solution)/shard_map/modes_to_field/pallas_call | solution.py:259
  (2 shorter events, 0.0 us)
Async XLA Ops:
  0.6 27.5 %copy-start = (bf16[64,64]{1,0:T(8,128)(2,1)S(1)}, bf16[64,64]{1,0:T(8,128)(2,1)}, u32[]{:S(2)}) copy-start(bf16[64,64]{1,0:T(8,128)(2,1)} %param.20) | copy-start | bytes 24580
  0.7 29.5 %copy-start.8 = (bf16[1,2048]{1,0:T(2,128)(2,1)S(1)}, bf16[1,2048]{1,0:T(2,128)(2,1)}, u32[]{:S(2)}) copy-start(bf16[1,2048]{1,0:T(2,128)(2,1)} %param.22) | copy-start | bytes 12292
  0.7 44.8 %copy-start.1 = (bf16[1,32,4096]{2,1,0:T(8,128)(2,1)S(1)}, bf16[1,32,4096]{2,1,0:T(8,128)(2,1)}, u32[]{:S(2)}) copy-start(bf16[1,32,4096]{2,1,0:T(8,128)(2,1)} %weight_ref.1) | copy-start | bytes 786436
  0.7 44.8 %copy-start.3 = (bf16[80,1024]{1,0:T(8,128)(2,1)S(1)}, bf16[80,1024]{1,0:T(8,128)(2,1)}, u32[]{:S(2)}) copy-start(bf16[80,1024]{1,0:T(8,128)(2,1)} %constant.36.clone.gather_ref) | copy-start | bytes 491524
  0.7 44.7 %copy-start.5 = (bf16[256,128]{1,0:T(8,128)(2,1)S(1)}, bf16[256,128]{1,0:T(8,128)(2,1)}, u32[]{:S(2)}) copy-start(bf16[256,128]{1,0:T(8,128)(2,1)} %constant.37.clone.halves_ref) | copy-start | bytes 196612
  0.7 44.7 %copy-start.6 = (bf16[128,64]{1,0:T(8,128)(2,1)S(1)}, bf16[128,64]{1,0:T(8,128)(2,1)}, u32[]{:S(2)}) copy-start(bf16[128,64]{1,0:T(8,128)(2,1)} %constant.38.clone.spread_ref) | copy-start | bytes 49156
  5.9 66.5 %copy-start.2 = (bf16[80,1024]{1,0:T(8,128)(2,1)S(1)}, bf16[80,1024]{1,0:T(8,128)(2,1)}, u32[]{:S(2)}) copy-start(bf16[80,1024]{1,0:T(8,128)(2,1)} %constant.40.clone.pick_ref) | copy-start | bytes 491524
  6.0 66.5 %copy-start.4 = (bf16[256,128]{1,0:T(8,128)(2,1)S(1)}, bf16[256,128]{1,0:T(8,128)(2,1)}, u32[]{:S(2)}) copy-start(bf16[256,128]{1,0:T(8,128)(2,1)} %constant.41.clone.radial_ref) | copy-start | bytes 196612
  6.0 66.5 %copy-start.7 = (f32[16,256]{1,0:T(8,128)S(1)}, f32[16,256]{1,0:T(8,128)}, u32[]{:S(2)}) copy-start(f32[16,256]{1,0:T(8,128)} %constant.42.clone.same_ref) | copy-start | bytes 49156
  6.0 39.4 %all-to-all-start = ((bf16[512,2,128]{2,1,0:T(2,128)(2,1)}), bf16[512,2,128]{2,1,0:T(2,128)(2,1)S(1)}, u32[]{:S(2)}, u32[]{:S(2)}) async-start(bf16[512,2,128]{2,1,0:T(2,128)(2,1)} %bitcast.18), calls=%async_computation | async-start | bytes 524288 | tf_op jit(solution)/shard_map/all_to_all | solution.py:281
  46.9 25.5 %all-to-all-start.1 = ((bf16[512,2,128]{2,1,0:T(2,128)(2,1)}), bf16[512,2,128]{2,1,0:T(2,128)(2,1)S(1)}, u32[]{:S(2)}, u32[]{:S(2)}) async-start(bf16[512,2,128]{2,1,0:T(2,128)(2,1)} %bitcast.3), calls=%async_computation.1 | async-start | bytes 524288 | tf_op jit(solution)/shard_map/all_to_all | solution.py:281

commit v4 on v3

--- a/solution.py
+++ b/solution.py
@@ -103,88 +103,90 @@
     return jnp.where(lane < 64, high, pltpu.roll(values - high, 64, 1))
 
 
-def first_kernel(where, swap_ref, ends_ref, layer_hbm, pre_hbm, grad_hbm, place_hbm, forward_hbm,
-                 slope_hbm, sent_ref, layer, pre, grad, slope, layer_rows, grad_rows, coefs, place, forward,
-                 in_sem, out_sem, table_sem):
-    chunks = in_sem.shape[0]
-    group = CH // chunks
+def first_kernel(layer_hbm, pre_hbm, grad_hbm, swap_hbm, ends_hbm, place_hbm, forward_hbm,
+                 slope_hbm, sent_hbm, layer, pre, grad, slope, layer_rows, grad_rows, coefs,
+                 swap, ends, place, forward, sent, in_sem, out_sem, table_sem, sent_sem):
+    chunks, blocks = in_sem.shape[0], sent_sem.shape[0]
+    group, size = CH // chunks, sent.shape[0] // blocks
     copies = []
     for c in range(chunks):
         part = pl.ds(c * group, group)
         pairs = ((pre_hbm, pre), (grad_hbm, grad), (layer_hbm, layer))
         copies.append([pltpu.make_async_copy(a.at[part], b.at[part], in_sem.at[c, n]) for n, (a, b) in enumerate(pairs)])
-        for copy in copies[-1]:
-            copy.start()
-    tables = [
-        pltpu.make_async_copy(forward_hbm.at[where[0]], forward, table_sem.at[0]),
-        pltpu.make_async_copy(place_hbm, place, table_sem.at[1]),
-    ]
-    for copy in tables:
+    pairs = ((swap_hbm, swap), (ends_hbm, ends), (place_hbm, place), (forward_hbm.at[lax.axis_index("az")], forward))
+    tables = [pltpu.make_async_copy(a, b, table_sem.at[n]) for n, (a, b) in enumerate(pairs)]
+    for copy in copies[0] + tables[:1] + sum(copies[1:], []) + tables[1:]:
         copy.start()
-    swap = swap_ref[...]
     leaving = []
     for c in range(chunks):
         part = pl.ds(c * group, group)
-        for copy in copies[c]:
-            copy.wait()
+        copies[c][0].wait()
+        copies[c][1].wait()
         slope[part] = (grad[part].astype(F32) * gelu_slope(pre[part].astype(F32))).astype(BF)
         leaving.append(pltpu.make_async_copy(slope.at[part], slope_hbm.at[part], out_sem.at[c]))
         leaving[-1].start()
+        copies[c][2].wait()
+        if c == 0:
+            tables[0].wait()
         for at in range(c * group, (c + 1) * group, 16):
             for x in range(2):
                 both = jnp.concatenate(
                     [layer[at : at + 16, x].reshape(256, 128), slope[at : at + 16, x].reshape(256, 128)], axis=1
                 )
-                moved = dot_nn(swap, both).astype(BF)
+                moved = dot_nn(swap[...], both).astype(BF)
                 rows = slice(x * CH + at, x * CH + at + 16)
                 layer_rows[:, rows, :] = moved[:, :128].reshape(16, 16, 128)
                 grad_rows[:, rows, :] = moved[:, 128:].reshape(16, 16, 128)
+    for copy in tables[1:]:
+        copy.wait()
     point = jnp.zeros((128, 128), F32)
     bias = jnp.zeros((16, 128), F32)
     for t in range(16):
-        left = jnp.concatenate([layer_rows[t], ends_ref[...]], axis=0)
+        left = jnp.concatenate([layer_rows[t], ends[...]], axis=0)
         out = dot_nt(left, grad_rows[t])
         point += out[:128]
         coefs[t * MR : (t + 1) * MR, :] = out[128:144].astype(BF)
         bias += out[144:]
     point = point[:64] + pltpu.roll(point[64:], 64, 1)
     bias = bias + pltpu.roll(bias, 64, 1)
-    sums = jnp.concatenate([split_halves(point), split_halves(bias), jnp.zeros((48, 128), F32)], axis=0)
-    for copy in tables:
-        copy.wait()
-    sent = dot_nn(forward[...], coefs[...]) + dot_nn(place[...], sums.astype(BF))
-    sent_ref[...] = sent.astype(BF)
+    sums = jnp.concatenate([split_halves(point), split_halves(bias), jnp.zeros((48, 128), F32)], axis=0).astype(BF)
+    coef = coefs[...]
+    for b in range(blocks):
+        rows = slice(b * size, (b + 1) * size)
+        sent[rows] = (dot_nn(forward[rows], coef) + dot_nn(place[rows], sums)).astype(BF)
+        leaving.append(pltpu.make_async_copy(sent.at[rows], sent_hbm.at[rows], sent_sem.at[b]))
+        leaving[-1].start()
     for copy in leaving:
         copy.wait()
 
 
 def first(layer_input, pre_act, out_grad, tables):
-    chunks = 2
+    chunks, blocks = 2, 2
     shape = (CH, 2, 16, 128)
-    where = lax.axis_index("az").astype(jnp.int32).reshape(1)
-    hbm, vmem = pl.BlockSpec(memory_space=pl.ANY), pl.BlockSpec(memory_space=pltpu.VMEM)
+    hbm = pl.BlockSpec(memory_space=pl.ANY)
     return pl.pallas_call(
         first_kernel,
-        in_specs=[pl.BlockSpec(memory_space=pltpu.SMEM), vmem, vmem, hbm, hbm, hbm, hbm, hbm],
-        out_specs=[hbm, vmem],
-        scratch_shapes=[
-            pltpu.VMEM(shape, BF),
-            pltpu.VMEM(shape, BF),
-            pltpu.VMEM(shape, BF),
-            pltpu.VMEM(shape, BF),
+        in_specs=[hbm] * 7,
+        out_specs=[hbm] * 2,
+        scratch_shapes=[pltpu.VMEM(shape, BF)] * 4
+        + [
             pltpu.VMEM((16, 128, 128), BF),
             pltpu.VMEM((16, 128, 128), BF),
             pltpu.VMEM((256, 128), BF),
+            pltpu.VMEM((256, 256), BF),
+            pltpu.VMEM((32, 128), BF),
             pltpu.VMEM((1024, 128), BF),
             pltpu.VMEM((1024, 256), BF),
+            pltpu.VMEM((1024, 128), BF),
             pltpu.SemaphoreType.DMA((chunks, 3)),
             pltpu.SemaphoreType.DMA((chunks,)),
-            pltpu.SemaphoreType.DMA((2,)),
+            pltpu.SemaphoreType.DMA((4,)),
+            pltpu.SemaphoreType.DMA((blocks,)),
         ],
         out_shape=[jax.ShapeDtypeStruct(shape, BF), jax.ShapeDtypeStruct((1024, 128), BF)],
         compiler_params=pltpu.CompilerParams(vmem_limit_bytes=60 * 1024 * 1024),
         name="slope_and_modes",
-    )(where, tables["swap"], tables["ends"], layer_input, pre_act, out_grad, tables["place"], tables["forward"])
+    )(layer_input, pre_act, out_grad, tables["swap"], tables["ends"], tables["place"], tables["forward"])
 
 
 def middle_kernel(gain, norm, got_ref, gather_ref, weight_ref, halves_ref, spread_ref, mode_ref, sent_ref, stack):
@@ -224,14 +226,23 @@
 
 
 def last_kernel(got_ref, pick_ref, radial_ref, same_ref, inverse_ref, point_ref,
-                field_hbm, weight_ref, bias_ref, columns, wide, field, out_sem):
+                field_hbm, weight_hbm, bias_hbm, columns, wide, field, weight, bias, out_sem, sums_sem):
     got = got_ref[...]
+    sums = dot_nn(pick_ref[...], got)
+    sums = sums + pltpu.roll(sums, 64, 1)
+    weight[...] = sums[:64, :64]
+    bias[...] = sums[64, :64]
+    leaving = [
+        pltpu.make_async_copy(weight, weight_hbm, sums_sem.at[0]),
+        pltpu.make_async_copy(bias, bias_hbm, sums_sem.at[1]),
+    ]
+    for copy in leaving:
+        copy.start()
     columns[...] = jnp.transpose(dot_nn(inverse_ref[...], got))
     same = same_ref[...]
     radial = radial_ref[...]
     chunks = out_sem.shape[0]
     group = CH // chunks
-    leaving = []
     for c in range(chunks):
         for at in range(group):
             for x in range(2):
@@ -244,10 +255,6 @@
         field[part] = (spectral.reshape(group, 2, 16, 128) + point_ref[part]).astype(BF)
         leaving.append(pltpu.make_async_copy(field.at[part], field_hbm.at[part], out_sem.at[c]))
         leaving[-1].start()
-    sums = dot_nn(pick_ref[...], got)
-    sums = sums + pltpu.roll(sums, 64, 1)
-    weight_ref[...] = sums[:64, :64]
-    bias_ref[...] = sums[64, :64]
     for copy in leaving:
         copy.wait()
 
@@ -259,12 +266,15 @@
     return pl.pallas_call(
         last_kernel,
         in_specs=[vmem] * 6,
-        out_specs=[hbm, vmem, vmem],
+        out_specs=[hbm] * 3,
         scratch_shapes=[
             pltpu.VMEM((128, 256), F32),
             pltpu.VMEM((chunks, CH // chunks * 32, 256), BF),
             pltpu.VMEM(shape, BF),
+            pltpu.VMEM((CH, CH), F32),
+            pltpu.VMEM((CH,), F32),
             pltpu.SemaphoreType.DMA((chunks,)),
+            pltpu.SemaphoreType.DMA((2,)),
         ],
         out_shape=[
             jax.ShapeDtypeStruct(shape, BF),

time: 74.9 us -> 73.5 us (0.981)
  Pallas kernels: 8.8 us -> 7.45 us
    pallas_call x2, Pallas kernels: 7.33 us -> 5.98 us  [the longest x1 4.43 us: first(): pl.pallas_call(first_kernel, in_specs=[hbm] * 7, out_specs=[hbm] * 2, scr...]
where the time goes in v4:
time: 73.5 us; the launch traced here: 73.2 us
  starting transfers between devices  30.5 us (41%)
  waiting for transfers between devices  29.7 us (40%)
  Pallas kernels  7.45 us (10%)
  local copies, waits for them, and re-layouts  2.99 us (4%)
  matrix products  1.34 us (2%)
  between operations  0.8 us (1%)
    all_to_all x2, starting transfers between devices, exchange(): lax.all_to_all(sent, ('az', 'ax'), 0, 0, tiled=True)  30.5 us
    all_to_all x2, waiting for transfers between devices, exchange(): lax.all_to_all(sent, ('az', 'ax'), 0, 0, tiled=True)  29.7 us
    pallas_call x1, Pallas kernels, first(): pl.pallas_call(first_kernel, in_specs=[hbm] * 7, out_specs=[hbm] * 2, scr...  4.43 us
    pallas_call x1, Pallas kernels, last(): pl.pallas_call(last_kernel, in_specs=[vmem] * 6, out_specs=[hbm] * 3, scr...  1.55 us
  transfers between devices with their start and end apart: 2, of which 2 were waited for; matrix products, arithmetic and copies ran while one was open for 6% of the time, Pallas kernels for 0%

profile of v4, /device:TPU:1, one launch (start us, length us, event | category | flops | bytes accessed | tf_op | source)
XLA Modules:
  0.0 73.2 jit_solution(448268708272281264)
XLA Ops:
  0.6 0.0 copy-start
  0.6 0.0 copy-start.3
  0.7 0.0 copy-start.5
  0.7 0.0 copy-start.6
  0.7 0.0 copy-start.8
  0.7 0.0 copy-start.1
  0.7 4.4 %slope_and_modes.1 = (bf16[64,2,16,128]{3,2,1,0:T(8,128)(2,1)}, bf16[1024,128]{1,0:T(8,128)(2,1)}) custom-call(bf16[64,2,16,128]{3,2,1,0:T(8,128)(2,1)} %layer_hbm.1, bf16[64,2,16,128]{3,2,1,0:T(8,128)(2,1)} %pre_hbm.1, bf16[64,2,16,128]{3,2,1,0:T(8,128)(2,1)} %grad_hbm.1, bf16[256,256]{1,0:T(8,128)(2,1)} %constant.32.clone.swap_hbm, ...), custom_call_target="tpu_custom_call" | custom-call | tf_op jit(solution)/shard_map/slope_and_modes/pallas_call | solution.py:167
  5.1 0.0 copy-start.2
  5.2 0.0 copy-start.4
  5.2 0.0 copy-start.7
  5.2 22.2 %all-to-all-start = ((bf16[512,2,128]{2,1,0:T(2,128)(2,1)}), bf16[512,2,128]{2,1,0:T(2,128)(2,1)S(1)}, u32[]{:S(2)}, u32[]{:S(2)}) async-start(bf16[512,2,128]{2,1,0:T(2,128)(2,1)} %bitcast.17), calls=%async_computation | async-start | bytes 524288 | tf_op jit(solution)/shard_map/all_to_all | solution.py:291
  27.4 0.0 copy-done
  27.4 1.3 %fusion = f32[2,16,128,64]{2,3,1,0:T(8,128)S(1)} fusion(bf16[64,2,16,128]{3,2,1,0:T(8,128)(2,1)} %get-tuple-element.16, bf16[64,64]{1,0:T(8,128)(2,1)S(1)} %copy-done), kind=kOutput, calls=%fused_computation.2 | convolution fusion | flops 33554432 | bytes 1581056 | tf_op jit(solution)/shard_map/io,oxtr->ixtr/dot_general | solution.py:316
  28.7 0.6 copy.27
  29.3 0.0 copy-done.8
  29.4 0.1 reshape.56
  29.4 15.2 %all-to-all-done = bf16[512,2,128]{2,1,0:T(2,128)(2,1)S(1)} async-done(((bf16[512,2,128]{2,1,0:T(2,128)(2,1)}), bf16[512,2,128]{2,1,0:T(2,128)(2,1)S(1)}, u32[]{:S(2)}, u32[]{:S(2)}) %all-to-all-start) | async-done | bytes 262176 | tf_op jit(solution)/shard_map/all_to_all | solution.py:291
  44.6 0.0 copy-done.3
  44.6 0.0 copy-done.5
  44.6 0.0 copy-done.6
  44.6 0.0 copy-done.1
  44.6 1.5 %modes_and_mixing.1 = (bf16[32,128]{1,0:T(8,128)(2,1)S(1)}, bf16[8,128,128]{2,1,0:T(8,128)(2,1)}) custom-call(bf16[1024,128]{1,0:T(8,128)(2,1)S(1)} %bitcast.15, bf16[80,1024]{1,0:T(8,128)(2,1)S(1)} %copy-done.3, bf16[1,32,4096]{2,1,0:T(8,128)(2,1)S(1)} %copy-done.1, bf16[256,128]{1,0:T(8,128)(2,1)S(1)} %copy-done.5, bf16[128,64]{1,0:T(8,128)(2,1)S(1)} %copy-done.6), custom_call_target="tpu_custom_call" | custom-call | tf_op jit(solution)/shard_map/modes_and_mixing/pallas_call | solution.py:219
  46.1 8.3 %all-to-all-start.1 = ((bf16[512,2,128]{2,1,0:T(2,128)(2,1)}), bf16[512,2,128]{2,1,0:T(2,128)(2,1)S(1)}, u32[]{:S(2)}, u32[]{:S(2)}) async-start(bf16[512,2,128]{2,1,0:T(2,128)(2,1)} %bitcast.2), calls=%async_computation.1 | async-start | bytes 524288 | tf_op jit(solution)/shard_map/all_to_all | solution.py:291
  54.5 0.3 multiply_convert_fusion
  54.8 1.2 %convert_element_type.30 = bf16[1,32,4096]{2,1,0:T(8,128)(2,1)} reshape(bf16[32,64,64]{2,1,0:T(8,128)(2,1)S(1)} %multiply_convert_fusion) | data formatting | bytes 524288 | tf_op jit(solution)/shard_map/convert_element_type | solution.py:312
  56.0 1.1 %dynamic-slice_bitcast_fusion.inverse_ref = bf16[256,1024]{1,0:T(8,128)(2,1)S(1)} fusion(bf16[8,256,1024]{2,1,0:T(8,128)(2,1)} %constant.39.clone, s32[]{:T(128)S(6)} %select_n.4), kind=kLoop, calls=%fused_computation.4 | loop fusion | bytes 1048580 | tf_op jit(solution)/shard_map/jit(dynamic_index_in_dim)/squeeze | solution.py:315
  57.1 14.6 %all-to-all-done.1 = bf16[512,2,128]{2,1,0:T(2,128)(2,1)S(1)} async-done(((bf16[512,2,128]{2,1,0:T(2,128)(2,1)}), bf16[512,2,128]{2,1,0:T(2,128)(2,1)S(1)}, u32[]{:S(2)}, u32[]{:S(2)}) %all-to-all-start.1) | async-done | bytes 262176 | tf_op jit(solution)/shard_map/all_to_all | solution.py:291
  71.6 0.0 copy-done.2
  71.7 0.0 copy-done.4
  71.7 0.0 copy-done.7
  71.7 1.6 %modes_to_field.1 = (bf16[64,2,16,128]{3,2,1,0:T(8,128)(2,1)}, f32[64,64]{1,0:T(8,128)}, f32[64]{0:T(128)}) custom-call(bf16[1024,128]{1,0:T(8,128)(2,1)S(1)} %bitcast.16, bf16[80,1024]{1,0:T(8,128)(2,1)S(1)} %copy-done.2, bf16[256,128]{1,0:T(8,128)(2,1)S(1)} %copy-done.4, f32[16,256]{1,0:T(8,128)S(1)} %copy-done.7, ...), custom_call_target="tpu_custom_call" | custom-call | tf_op jit(solution)/shard_map/modes_to_field/pallas_call | solution.py:266
  (2 shorter events, 0.0 us)
Async XLA Ops:
  0.6 26.7 %copy-start = (bf16[64,64]{1,0:T(8,128)(2,1)S(1)}, bf16[64,64]{1,0:T(8,128)(2,1)}, u32[]{:S(2)}) copy-start(bf16[64,64]{1,0:T(8,128)(2,1)} %param.20) | copy-start | bytes 24580
  0.6 44.0 %copy-start.3 = (bf16[80,1024]{1,0:T(8,128)(2,1)S(1)}, bf16[80,1024]{1,0:T(8,128)(2,1)}, u32[]{:S(2)}) copy-start(bf16[80,1024]{1,0:T(8,128)(2,1)} %constant.36.clone.gather_ref) | copy-start | bytes 491524
  0.7 44.0 %copy-start.5 = (bf16[256,128]{1,0:T(8,128)(2,1)S(1)}, bf16[256,128]{1,0:T(8,128)(2,1)}, u32[]{:S(2)}) copy-start(bf16[256,128]{1,0:T(8,128)(2,1)} %constant.37.clone.halves_ref) | copy-start | bytes 196612
  0.7 44.0 %copy-start.6 = (bf16[128,64]{1,0:T(8,128)(2,1)S(1)}, bf16[128,64]{1,0:T(8,128)(2,1)}, u32[]{:S(2)}) copy-start(bf16[128,64]{1,0:T(8,128)(2,1)} %constant.38.clone.spread_ref) | copy-start | bytes 49156
  0.7 28.7 %copy-start.8 = (bf16[1,2048]{1,0:T(2,128)(2,1)S(1)}, bf16[1,2048]{1,0:T(2,128)(2,1)}, u32[]{:S(2)}) copy-start(bf16[1,2048]{1,0:T(2,128)(2,1)} %param.22) | copy-start | bytes 12292
  0.7 43.9 %copy-start.1 = (bf16[1,32,4096]{2,1,0:T(8,128)(2,1)S(1)}, bf16[1,32,4096]{2,1,0:T(8,128)(2,1)}, u32[]{:S(2)}) copy-start(bf16[1,32,4096]{2,1,0:T(8,128)(2,1)} %weight_ref.1) | copy-start | bytes 786436
  5.1 66.5 %copy-start.2 = (bf16[80,1024]{1,0:T(8,128)(2,1)S(1)}, bf16[80,1024]{1,0:T(8,128)(2,1)}, u32[]{:S(2)}) copy-start(bf16[80,1024]{1,0:T(8,128)(2,1)} %constant.40.clone.pick_ref) | copy-start | bytes 491524
  5.2 66.5 %copy-start.4 = (bf16[256,128]{1,0:T(8,128)(2,1)S(1)}, bf16[256,128]{1,0:T(8,128)(2,1)}, u32[]{:S(2)}) copy-start(bf16[256,128]{1,0:T(8,128)(2,1)} %constant.41.clone.radial_ref) | copy-start | bytes 196612
  5.2 66.5 %copy-start.7 = (f32[16,256]{1,0:T(8,128)S(1)}, f32[16,256]{1,0:T(8,128)}, u32[]{:S(2)}) copy-start(f32[16,256]{1,0:T(8,128)} %constant.42.clone.same_ref) | copy-start | bytes 49156
  5.2 39.4 %all-to-all-start = ((bf16[512,2,128]{2,1,0:T(2,128)(2,1)}), bf16[512,2,128]{2,1,0:T(2,128)(2,1)S(1)}, u32[]{:S(2)}, u32[]{:S(2)}) async-start(bf16[512,2,128]{2,1,0:T(2,128)(2,1)} %bitcast.17), calls=%async_computation | async-start | bytes 524288 | tf_op jit(solution)/shard_map/all_to_all | solution.py:291
  46.1 25.5 %all-to-all-start.1 = ((bf16[512,2,128]{2,1,0:T(2,128)(2,1)}), bf16[512,2,128]{2,1,0:T(2,128)(2,1)S(1)}, u32[]{:S(2)}, u32[]{:S(2)}) async-start(bf16[512,2,128]{2,1,0:T(2,128)(2,1)} %bitcast.2), calls=%async_computation.1 | async-start | bytes 524288 | tf_op jit(solution)/shard_map/all_to_all | solution.py:291

commit v5 on v4

--- a/solution.py
+++ b/solution.py
@@ -7,6 +7,7 @@
 from jax import lax
 from jax.experimental import pallas as pl
 from jax.experimental.pallas import tpu as pltpu
+from jax.sharding import Mesh
 from jax.sharding import PartitionSpec as P
 
 CH = 64
@@ -57,7 +58,6 @@
         forward[:, :, k, 0, :, k] = part.transpose(0, 2, 1)
     forward = forward.reshape(cycle_devices, 2 * pairs, sector * MR)
     tables["forward"] = forward
-    tables["inverse"] = forward.transpose(0, 2, 1)
     rows = np.zeros((pairs, 2, 128), np.float32)
     for p in range(pairs):
         rows[p, 1, CH if p % 8 == 7 else p // 8] = 1.0
@@ -66,7 +66,12 @@
     for i in range(CH):
         pick[i, 8 * i, 1] = 1.0
     pick[CH, 7, 1] = 1.0
-    tables["pick"] = pick.reshape(80, 2 * pairs)
+    inverse = np.concatenate(
+        [forward.transpose(0, 2, 1), np.broadcast_to(pick.reshape(1, 80, 2 * pairs), (cycle_devices, 80, 2 * pairs))], axis=1
+    )
+    inverse = inverse.reshape(cycle_devices, 336, cycle_devices // 2, 2, 2 * pairs // cycle_devices)
+    inverse = np.stack([inverse[az][:, :, [az % 2, 1 - az % 2]] for az in range(cycle_devices)])
+    tables["inverse"] = inverse.transpose(0, 1, 3, 2, 4).reshape(cycle_devices, 336, 2 * pairs)
     gather = np.zeros((80, cycle_devices, pairs // cycle_devices, 2), np.float32)
     ax_devices = pairs // cycle_devices
     slab = axial // ax_devices
@@ -84,6 +89,10 @@
     return {name: value.astype(jnp.float32 if name == "same" else jnp.bfloat16) for name, value in tables.items()}
 
 
+def cycle_index():
+    return lax.axis_index("y_hi") * 2 + lax.axis_index("core")
+
+
 def gelu_slope(values):
     density = jnp.exp(-0.5 * values * values) * (1.0 / math.sqrt(2.0 * math.pi))
     return 0.5 * (1.0 + lax.erf(values * (1.0 / math.sqrt(2.0)))) + values * density
@@ -113,7 +122,7 @@
         part = pl.ds(c * group, group)
         pairs = ((pre_hbm, pre), (grad_hbm, grad), (layer_hbm, layer))
         copies.append([pltpu.make_async_copy(a.at[part], b.at[part], in_sem.at[c, n]) for n, (a, b) in enumerate(pairs)])
-    pairs = ((swap_hbm, swap), (ends_hbm, ends), (place_hbm, place), (forward_hbm.at[lax.axis_index("az")], forward))
+    pairs = ((swap_hbm, swap), (ends_hbm, ends), (place_hbm, place), (forward_hbm.at[cycle_index()], forward))
     tables = [pltpu.make_async_copy(a, b, table_sem.at[n]) for n, (a, b) in enumerate(pairs)]
     for copy in copies[0] + tables[:1] + sum(copies[1:], []) + tables[1:]:
         copy.start()
@@ -211,25 +220,25 @@
     sums = split_halves((sums + pltpu.roll(sums, 64, 1)) * norm)
     row = lax.broadcasted_iota(jnp.int32, (128, 128), 0)
     slabs = jnp.where(row % 2 == 0, slabs, sums[:1]).astype(BF)
-    for az in range(8):
-        sent_ref[az] = slabs
+    for y_hi in range(4):
+        sent_ref[y_hi] = slabs
 
 
 def middle(got, spec_weight, tables, gain, norm):
     return pl.pallas_call(
         functools.partial(middle_kernel, gain, norm),
-        out_shape=[jax.ShapeDtypeStruct((32, 128), BF), jax.ShapeDtypeStruct((8, 128, 128), BF)],
+        out_shape=[jax.ShapeDtypeStruct((32, 128), BF), jax.ShapeDtypeStruct((4, 128, 128), BF)],
         scratch_shapes=[pltpu.VMEM((1024, 256), BF)],
         compiler_params=pltpu.CompilerParams(vmem_limit_bytes=VMEM_LIMIT),
         name="modes_and_mixing",
     )(got, tables["gather"], spec_weight, tables["halves"], tables["spread"])
 
 
-def last_kernel(got_ref, pick_ref, radial_ref, same_ref, inverse_ref, point_ref,
+def last_kernel(own_ref, other_ref, radial_ref, same_ref, inverse_ref, point_ref,
                 field_hbm, weight_hbm, bias_hbm, columns, wide, field, weight, bias, out_sem, sums_sem):
-    got = got_ref[...]
-    sums = dot_nn(pick_ref[...], got)
-    sums = sums + pltpu.roll(sums, 64, 1)
+    half = own_ref.shape[0]
+    out = dot_nn(inverse_ref[:, :half], own_ref[...]) + dot_nn(inverse_ref[:, half:], other_ref[...])
+    sums = out[256:] + pltpu.roll(out[256:], 64, 1)
     weight[...] = sums[:64, :64]
     bias[...] = sums[64, :64]
     leaving = [
@@ -238,7 +247,7 @@
     ]
     for copy in leaving:
         copy.start()
-    columns[...] = jnp.transpose(dot_nn(inverse_ref[...], got))
+    columns[...] = jnp.transpose(out[:256])
     same = same_ref[...]
     radial = radial_ref[...]
     chunks = out_sem.shape[0]
@@ -259,7 +268,7 @@
         copy.wait()
 
 
-def last(got, inverse, point_part, tables):
+def last(own, other, inverse, point_part, tables):
     chunks = 4
     shape = (CH, 2, 16, 128)
     hbm, vmem = pl.BlockSpec(memory_space=pl.ANY), pl.BlockSpec(memory_space=pltpu.VMEM)
@@ -283,18 +292,17 @@
         ],
         compiler_params=pltpu.CompilerParams(vmem_limit_bytes=32 * 1024 * 1024),
         name="modes_to_field",
-    )(got, tables["pick"], tables["radial"], tables["same"], inverse, point_part)
-
-
-def exchange(rows, devices):
-    sent = rows.reshape(devices, 2, 128)
-    return lax.all_to_all(sent, ("az", "ax"), 0, 0, tiled=True).reshape(2 * devices, 128)
+    )(own, other, tables["radial"], tables["same"], inverse, point_part)
+
+
+def exchange(rows, axes):
+    sent = rows.reshape(-1, 2, 128)
+    return lax.all_to_all(sent, axes, 0, 0, tiled=True).reshape(-1, 128)
 
 
 def per_device(layer_input, pre_act, out_grad, point_weight, spec_weight, saved_coeffs):
     axial_devices = lax.axis_size("ax")
-    cycle_devices = lax.axis_size("az")
-    devices = axial_devices * cycle_devices
+    cycle_devices = lax.axis_size(("y_hi", "core"))
     axial_total = layer_input.shape[1] * axial_devices
     cycle_total = layer_input.shape[2] * cycle_devices
     radial_length = layer_input.shape[3]
@@ -304,32 +312,29 @@
     tables = make_tables(axial_total, cycle_total, radial_length, cycle_devices)
 
     grad_pre, sent = first(layer_input, pre_act, out_grad, tables)
-    got = exchange(sent, devices)
+    got = exchange(sent, ("y_hi", "core", "ax"))
     mode_grad, sent = middle(got, spec_weight, tables, gain, norm)
-    got = exchange(sent.reshape(2 * devices, 128), devices)
+    own = exchange(sent, ("y_hi", "ax"))
     saved_modes = saved_coeffs.reshape(MX, CH).astype(F32)
     spec_grad = (
         (saved_modes[:, :, None] * mode_grad[:, :CH].astype(F32)[:, None, :]).astype(BF).reshape(1, MX, CH * CH)
     )
     inverse, _ = lax.optimization_barrier((tables["inverse"], mode_grad))
-    inverse = lax.dynamic_index_in_dim(inverse, lax.axis_index("az"), 0, keepdims=False)
+    inverse = lax.dynamic_index_in_dim(inverse, cycle_index(), 0, keepdims=False)
     point_part = jnp.einsum("io,oxtr->ixtr", point_weight, grad_pre, preferred_element_type=F32)
-    input_grad, point_grad, bias_grad = last(got, inverse, point_part, tables)
+    own, inverse, point_part, spec_grad = lax.optimization_barrier((own, inverse, point_part, spec_grad))
+    other = lax.ppermute(own, "core", [(0, 1), (1, 0)])
+    input_grad, point_grad, bias_grad = last(own, other, inverse, point_part, tables)
     return (input_grad, point_grad, bias_grad, spec_grad)
 
 
 def solution(mesh):
+    by_core = Mesh(mesh.devices.reshape(mesh.devices.shape[0], -1, 2), ("ax", "y_hi", "core"))
+    field = P(None, "ax", ("y_hi", "core"), None)
     return jax.shard_map(
         per_device,
-        mesh=mesh,
-        in_specs=(
-            P(None, "ax", "az", None),
-            P(None, "ax", "az", None),
-            P(None, "ax", "az", None),
-            P(),
-            P(("az", "ax"), None, None),
-            P(("az", "ax"), None),
-        ),
-        out_specs=(P(None, "ax", "az", None), P(), P(), P(("az", "ax"), None, None)),
+        mesh=by_core,
+        in_specs=(field, field, field, P(), P(("y_hi", "core", "ax"), None, None), P(("y_hi", "core", "ax"), None)),
+        out_specs=(field, P(), P(), P(("y_hi", "core", "ax"), None, None)),
         check_vma=False,
     )

time: 73.5 us -> 74.6 us (1.015)
  starting transfers between devices: 30.5 us -> 34.5 us
  waiting for transfers between devices: 29.7 us -> 26.5 us
    all_to_all x2, waiting for transfers between devices: 29.7 us -> 25.5 us  [exchange(): return lax.all_to_all(sent, axes, 0, 0, tiled=True).reshape(-1, 128)]
    ppermute x0 -> x1, starting transfers between devices: none -> 3.19 us  [per_device(): other = lax.ppermute(own, 'core', [(0, 1), (1, 0)])]
    ppermute x0 -> x1, waiting for transfers between devices: none -> 0.96 us  [per_device(): other = lax.ppermute(own, 'core', [(0, 1), (1, 0)])]
    all_to_all x2, starting transfers between devices: 30.5 us -> 31.3 us  [exchange(): return lax.all_to_all(sent, axes, 0, 0, tiled=True).reshape(-1, 128)]
  transfers between devices with their start and end apart: 2 -> 3, of which waited for: 2 -> 3; matrix products, arithmetic and copies ran while one was open for 6% -> 6% of each run, Pallas kernels for 0% -> 0%
where the time goes in v5:
time: 74.6 us; the launch traced here: 74.2 us
  starting transfers between devices  34.5 us (46%)
  waiting for transfers between devices  26.5 us (36%)
  Pallas kernels  7.63 us (10%)
  local copies, waits for them, and re-layouts  3.05 us (4%)
  matrix products  1.34 us (2%)
  between operations  0.8 us (1%)
    all_to_all x2, starting transfers between devices, exchange(): return lax.all_to_all(sent, axes, 0, 0, tiled=True).reshape(-1, 128)  31.3 us
    all_to_all x2, waiting for transfers between devices, exchange(): return lax.all_to_all(sent, axes, 0, 0, tiled=True).reshape(-1, 128)  25.5 us
    pallas_call x1, Pallas kernels, first(): pl.pallas_call(first_kernel, in_specs=[hbm] * 7, out_specs=[hbm] * 2, scr...  4.43 us
    ppermute x1, starting transfers between devices, per_device(): other = lax.ppermute(own, 'core', [(0, 1), (1, 0)])  3.19 us
    pallas_call x1, Pallas kernels, last(): pl.pallas_call(last_kernel, in_specs=[vmem] * 6, out_specs=[hbm] * 3, scr...  1.78 us
  transfers between devices with their start and end apart: 3, of which 3 were waited for; matrix products, arithmetic and copies ran while one was open for 6% of the time, Pallas kernels for 0%

profile of v5, /device:TPU:1, one launch (start us, length us, event | category | flops | bytes accessed | tf_op | source)
XLA Modules:
  0.0 74.2 jit_solution(13697544692598066726)
XLA Ops:
  0.6 0.0 copy-start
  0.6 0.0 copy-start.2
  0.7 0.0 copy-start.4
  0.7 0.0 copy-start.5
  0.7 0.0 copy-start.7
  0.7 0.0 copy-start.1
  0.7 4.4 %slope_and_modes.1 = (bf16[64,2,16,128]{3,2,1,0:T(8,128)(2,1)}, bf16[1024,128]{1,0:T(8,128)(2,1)}) custom-call(bf16[64,2,16,128]{3,2,1,0:T(8,128)(2,1)} %layer_hbm.1, bf16[64,2,16,128]{3,2,1,0:T(8,128)(2,1)} %pre_hbm.1, bf16[64,2,16,128]{3,2,1,0:T(8,128)(2,1)} %grad_hbm.1, bf16[256,256]{1,0:T(8,128)(2,1)} %constant.36.clone.swap_hbm, ...), custom_call_target="tpu_custom_call" | custom-call | tf_op jit(solution)/shard_map/slope_and_modes/pallas_call | solution.py:176
  5.1 0.0 copy-start.3
  5.2 0.0 copy-start.6
  5.2 22.2 %all-to-all-start = ((bf16[512,2,128]{2,1,0:T(2,128)(2,1)}), bf16[512,2,128]{2,1,0:T(2,128)(2,1)S(1)}, u32[]{:S(2)}, u32[]{:S(2)}) async-start(bf16[512,2,128]{2,1,0:T(2,128)(2,1)} %bitcast.18), calls=%async_computation | async-start | bytes 524288 | tf_op jit(solution)/shard_map/all_to_all | solution.py:300
  27.3 0.0 copy-done
  27.4 1.3 %fusion = f32[2,16,128,64]{2,3,1,0:T(8,128)S(1)} fusion(bf16[64,2,16,128]{3,2,1,0:T(8,128)(2,1)} %get-tuple-element.20, bf16[64,64]{1,0:T(8,128)(2,1)S(1)} %copy-done), kind=kOutput, calls=%fused_computation.3 | convolution fusion | flops 33554432 | bytes 1581056 | tf_op jit(solution)/shard_map/io,oxtr->ixtr/dot_general | solution.py:324
  28.7 0.6 copy.26
  29.3 0.0 copy-done.7
  29.4 0.1 reshape.60
  29.4 15.2 %all-to-all-done = bf16[512,2,128]{2,1,0:T(2,128)(2,1)S(1)} async-done(((bf16[512,2,128]{2,1,0:T(2,128)(2,1)}), bf16[512,2,128]{2,1,0:T(2,128)(2,1)S(1)}, u32[]{:S(2)}, u32[]{:S(2)}) %all-to-all-start) | async-done | bytes 262176 | tf_op jit(solution)/shard_map/all_to_all | solution.py:300
  44.6 0.0 copy-done.2
  44.6 0.0 copy-done.4
  44.6 0.0 copy-done.5
  44.6 0.0 copy-done.1
  44.6 1.4 %modes_and_mixing.1 = (bf16[32,128]{1,0:T(8,128)(2,1)S(1)}, bf16[4,128,128]{2,1,0:T(8,128)(2,1)}) custom-call(bf16[1024,128]{1,0:T(8,128)(2,1)S(1)} %bitcast.15, bf16[80,1024]{1,0:T(8,128)(2,1)S(1)} %copy-done.2, bf16[1,32,4096]{2,1,0:T(8,128)(2,1)S(1)} %copy-done.1, bf16[256,128]{1,0:T(8,128)(2,1)S(1)} %copy-done.4, bf16[128,64]{1,0:T(8,128)(2,1)S(1)} %copy-done.5), custom_call_target="tpu_custom_call" | custom-call | tf_op jit(solution)/shard_map/modes_and_mixing/pallas_call | solution.py:228
  46.1 9.1 %all-to-all-start.1 = ((bf16[256,2,128]{2,1,0:T(2,128)(2,1)}), bf16[256,2,128]{2,1,0:T(2,128)(2,1)S(1)}, u32[]{:S(2)}, u32[]{:S(2)}) async-start(bf16[256,2,128]{2,1,0:T(2,128)(2,1)} %bitcast.2), calls=%async_computation.1 | async-start | bytes 262144 | tf_op jit(solution)/shard_map/all_to_all | solution.py:300
  55.2 0.3 multiply_convert_fusion
  55.6 1.2 %convert_element_type.30 = bf16[1,32,4096]{2,1,0:T(8,128)(2,1)} reshape(bf16[32,64,64]{2,1,0:T(8,128)(2,1)S(1)} %multiply_convert_fusion) | data formatting | bytes 524288 | tf_op jit(solution)/shard_map/convert_element_type | solution.py:320
  56.7 1.1 %dynamic-slice_bitcast_fusion.inverse_ref = bf16[336,1024]{1,0:T(8,128)(2,1)S(1)} fusion(bf16[8,336,1024]{2,1,0:T(8,128)(2,1)} %constant.43.clone, s32[]{:T(128)S(6)} %select_n.4), kind=kLoop, calls=%fused_computation.2 | loop fusion | bytes 1376260 | tf_op jit(solution)/shard_map/jit(dynamic_index_in_dim)/squeeze | solution.py:323
  57.9 10.4 %all-to-all-done.1 = bf16[256,2,128]{2,1,0:T(2,128)(2,1)S(1)} async-done(((bf16[256,2,128]{2,1,0:T(2,128)(2,1)}), bf16[256,2,128]{2,1,0:T(2,128)(2,1)S(1)}, u32[]{:S(2)}, u32[]{:S(2)}) %all-to-all-start.1) | async-done | bytes 131104 | tf_op jit(solution)/shard_map/all_to_all | solution.py:300
  68.2 3.2 %collective-permute-start = (bf16[512,128]{1,0:T(8,128)(2,1)S(1)}, bf16[512,128]{1,0:T(8,128)(2,1)S(1)}, u32[]{:S(2)}, u32[]{:S(2)}) collective-permute-start(bf16[512,128]{1,0:T(8,128)(2,1)S(1)} %bitcast.16), channel_id=1, source_target_pairs={{0,1},{1,0},{2,3},{3,2},{4,5},{5,4},{6,7},{7,6},{8,9},{9,8},{10,11... | collective-permute-start | bytes 393224 | tf_op jit(solution)/shard_map/ppermute | solution.py:326
  71.4 1.0 %collective-permute-done.other_ref = bf16[512,128]{1,0:T(8,128)(2,1)S(1)} collective-permute-done((bf16[512,128]{1,0:T(8,128)(2,1)S(1)}, bf16[512,128]{1,0:T(8,128)(2,1)S(1)}, u32[]{:S(2)}, u32[]{:S(2)}) %collective-permute-start) | collective-permute-done | bytes 131104 | tf_op jit(solution)/shard_map/ppermute | solution.py:326
  72.4 0.0 copy-done.3
  72.4 0.0 copy-done.6
  72.4 1.8 %modes_to_field.1 = (bf16[64,2,16,128]{3,2,1,0:T(8,128)(2,1)}, f32[64,64]{1,0:T(8,128)}, f32[64]{0:T(128)}) custom-call(bf16[512,128]{1,0:T(8,128)(2,1)S(1)} %bitcast.17, bf16[512,128]{1,0:T(8,128)(2,1)S(1)} %collective-permute-done.other_ref, bf16[256,128]{1,0:T(8,128)(2,1)S(1)} %copy-done.3, f32[16,256]{1,0:T(8,128)S(1)} %copy-done.6, ...), custom_call_target="tpu_custom_call" | custom-call | tf_op jit(solution)/shard_map/modes_to_field/pallas_call | solution.py:275
  (2 shorter events, 0.0 us)
Async XLA Ops:
  0.6 26.7 %copy-start = (bf16[64,64]{1,0:T(8,128)(2,1)S(1)}, bf16[64,64]{1,0:T(8,128)(2,1)}, u32[]{:S(2)}) copy-start(bf16[64,64]{1,0:T(8,128)(2,1)} %param.19) | copy-start | bytes 24580
  0.6 44.0 %copy-start.2 = (bf16[80,1024]{1,0:T(8,128)(2,1)S(1)}, bf16[80,1024]{1,0:T(8,128)(2,1)}, u32[]{:S(2)}) copy-start(bf16[80,1024]{1,0:T(8,128)(2,1)} %constant.40.clone.gather_ref) | copy-start | bytes 491524
  0.7 44.0 %copy-start.4 = (bf16[256,128]{1,0:T(8,128)(2,1)S(1)}, bf16[256,128]{1,0:T(8,128)(2,1)}, u32[]{:S(2)}) copy-start(bf16[256,128]{1,0:T(8,128)(2,1)} %constant.41.clone.halves_ref) | copy-start | bytes 196612
  0.7 43.9 %copy-start.5 = (bf16[128,64]{1,0:T(8,128)(2,1)S(1)}, bf16[128,64]{1,0:T(8,128)(2,1)}, u32[]{:S(2)}) copy-start(bf16[128,64]{1,0:T(8,128)(2,1)} %constant.42.clone.spread_ref) | copy-start | bytes 49156
  0.7 28.6 %copy-start.7 = (bf16[1,2048]{1,0:T(2,128)(2,1)S(1)}, bf16[1,2048]{1,0:T(2,128)(2,1)}, u32[]{:S(2)}) copy-start(bf16[1,2048]{1,0:T(2,128)(2,1)} %param.21) | copy-start | bytes 12292
  0.7 43.9 %copy-start.1 = (bf16[1,32,4096]{2,1,0:T(8,128)(2,1)S(1)}, bf16[1,32,4096]{2,1,0:T(8,128)(2,1)}, u32[]{:S(2)}) copy-start(bf16[1,32,4096]{2,1,0:T(8,128)(2,1)} %weight_ref.1) | copy-start | bytes 786436
  5.1 67.3 %copy-start.3 = (bf16[256,128]{1,0:T(8,128)(2,1)S(1)}, bf16[256,128]{1,0:T(8,128)(2,1)}, u32[]{:S(2)}) copy-start(bf16[256,128]{1,0:T(8,128)(2,1)} %constant.44.clone.radial_ref) | copy-start | bytes 196612
  5.2 67.3 %copy-start.6 = (f32[16,256]{1,0:T(8,128)S(1)}, f32[16,256]{1,0:T(8,128)}, u32[]{:S(2)}) copy-start(f32[16,256]{1,0:T(8,128)} %constant.45.clone.same_ref) | copy-start | bytes 49156
  5.2 39.4 %all-to-all-start = ((bf16[512,2,128]{2,1,0:T(2,128)(2,1)}), bf16[512,2,128]{2,1,0:T(2,128)(2,1)S(1)}, u32[]{:S(2)}, u32[]{:S(2)}) async-start(bf16[512,2,128]{2,1,0:T(2,128)(2,1)} %bitcast.18), calls=%async_computation | async-start | bytes 524288 | tf_op jit(solution)/shard_map/all_to_all | solution.py:300
  46.1 22.2 %all-to-all-start.1 = ((bf16[256,2,128]{2,1,0:T(2,128)(2,1)}), bf16[256,2,128]{2,1,0:T(2,128)(2,1)S(1)}, u32[]{:S(2)}, u32[]{:S(2)}) async-start(bf16[256,2,128]{2,1,0:T(2,128)(2,1)} %bitcast.2), calls=%async_computation.1 | async-start | bytes 262144 | tf_op jit(solution)/shard_map/all_to_all | solution.py:300
  68.2 4.2 %collective-permute-start = (bf16[512,128]{1,0:T(8,128)(2,1)S(1)}, bf16[512,128]{1,0:T(8,128)(2,1)S(1)}, u32[]{:S(2)}, u32[]{:S(2)}) collective-permute-start(bf16[512,128]{1,0:T(8,128)(2,1)S(1)} %bitcast.16), channel_id=1, source_target_pairs={{0,1},{1,0},{2,3},{3,2},{4,5},{5,4},{6,7},{7,6},{8,9},{9,8},{10,11... | collective-permute-start | bytes 393224 | tf_op jit(solution)/shard_map/ppermute | solution.py:326

commit v6 on v4

--- a/solution.py
+++ b/solution.py
@@ -56,12 +56,12 @@
         part = cycle_all.reshape(cycle_devices, sector, 2 * MT)
         forward[:, :, k, 0, :, k] = part.transpose(0, 2, 1)
     forward = forward.reshape(cycle_devices, 2 * pairs, sector * MR)
-    tables["forward"] = forward
     tables["inverse"] = forward.transpose(0, 2, 1)
     rows = np.zeros((pairs, 2, 128), np.float32)
     for p in range(pairs):
         rows[p, 1, CH if p % 8 == 7 else p // 8] = 1.0
-    tables["place"] = rows.reshape(2 * pairs, 128)
+    place = np.broadcast_to(rows.reshape(1, 2 * pairs, 128), (cycle_devices, 2 * pairs, 128))
+    tables["forward"] = np.concatenate([forward, place], axis=2)
     pick = np.zeros((80, pairs, 2), np.float32)
     for i in range(CH):
         pick[i, 8 * i, 1] = 1.0
@@ -103,9 +103,9 @@
     return jnp.where(lane < 64, high, pltpu.roll(values - high, 64, 1))
 
 
-def first_kernel(layer_hbm, pre_hbm, grad_hbm, swap_hbm, ends_hbm, place_hbm, forward_hbm,
+def first_kernel(layer_hbm, pre_hbm, grad_hbm, swap_hbm, ends_hbm, forward_hbm,
                  slope_hbm, sent_hbm, layer, pre, grad, slope, layer_rows, grad_rows, coefs,
-                 swap, ends, place, forward, sent, in_sem, out_sem, table_sem, sent_sem):
+                 swap, ends, forward, sent, in_sem, out_sem, table_sem, sent_sem):
     chunks, blocks = in_sem.shape[0], sent_sem.shape[0]
     group, size = CH // chunks, sent.shape[0] // blocks
     copies = []
@@ -113,7 +113,7 @@
         part = pl.ds(c * group, group)
         pairs = ((pre_hbm, pre), (grad_hbm, grad), (layer_hbm, layer))
         copies.append([pltpu.make_async_copy(a.at[part], b.at[part], in_sem.at[c, n]) for n, (a, b) in enumerate(pairs)])
-    pairs = ((swap_hbm, swap), (ends_hbm, ends), (place_hbm, place), (forward_hbm.at[lax.axis_index("az")], forward))
+    pairs = ((swap_hbm, swap), (ends_hbm, ends), (forward_hbm.at[lax.axis_index("az")], forward))
     tables = [pltpu.make_async_copy(a, b, table_sem.at[n]) for n, (a, b) in enumerate(pairs)]
     for copy in copies[0] + tables[:1] + sum(copies[1:], []) + tables[1:]:
         copy.start()
@@ -139,21 +139,21 @@
                 grad_rows[:, rows, :] = moved[:, 128:].reshape(16, 16, 128)
     for copy in tables[1:]:
         copy.wait()
-    point = jnp.zeros((128, 128), F32)
+    point = dot_nt(
+        jnp.concatenate([layer_rows[t] for t in range(16)], axis=1), jnp.concatenate([grad_rows[t] for t in range(16)], axis=1)
+    )
+    out = dot_nt(ends[...], grad_rows[...].reshape(2048, 128))
     bias = jnp.zeros((16, 128), F32)
     for t in range(16):
-        left = jnp.concatenate([layer_rows[t], ends[...]], axis=0)
-        out = dot_nt(left, grad_rows[t])
-        point += out[:128]
-        coefs[t * MR : (t + 1) * MR, :] = out[128:144].astype(BF)
-        bias += out[144:]
+        coefs[t * MR : (t + 1) * MR, :] = out[:16, t * 128 : (t + 1) * 128].astype(BF)
+        bias += out[16:, t * 128 : (t + 1) * 128]
     point = point[:64] + pltpu.roll(point[64:], 64, 1)
     bias = bias + pltpu.roll(bias, 64, 1)
     sums = jnp.concatenate([split_halves(point), split_halves(bias), jnp.zeros((48, 128), F32)], axis=0).astype(BF)
-    coef = coefs[...]
+    coef = jnp.concatenate([coefs[...], sums], axis=0)
     for b in range(blocks):
         rows = slice(b * size, (b + 1) * size)
-        sent[rows] = (dot_nn(forward[rows], coef) + dot_nn(place[rows], sums)).astype(BF)
+        sent[rows] = dot_nn(forward[rows], coef).astype(BF)
         leaving.append(pltpu.make_async_copy(sent.at[rows], sent_hbm.at[rows], sent_sem.at[b]))
         leaving[-1].start()
     for copy in leaving:
@@ -166,7 +166,7 @@
     hbm = pl.BlockSpec(memory_space=pl.ANY)
     return pl.pallas_call(
         first_kernel,
-        in_specs=[hbm] * 7,
+        in_specs=[hbm] * 6,
         out_specs=[hbm] * 2,
         scratch_shapes=[pltpu.VMEM(shape, BF)] * 4
         + [
@@ -175,18 +175,17 @@
             pltpu.VMEM((256, 128), BF),
             pltpu.VMEM((256, 256), BF),
             pltpu.VMEM((32, 128), BF),
-            pltpu.VMEM((1024, 128), BF),
-            pltpu.VMEM((1024, 256), BF),
+            pltpu.VMEM((1024, 384), BF),
             pltpu.VMEM((1024, 128), BF),
             pltpu.SemaphoreType.DMA((chunks, 3)),
             pltpu.SemaphoreType.DMA((chunks,)),
-            pltpu.SemaphoreType.DMA((4,)),
+            pltpu.SemaphoreType.DMA((3,)),
             pltpu.SemaphoreType.DMA((blocks,)),
         ],
         out_shape=[jax.ShapeDtypeStruct(shape, BF), jax.ShapeDtypeStruct((1024, 128), BF)],
         compiler_params=pltpu.CompilerParams(vmem_limit_bytes=60 * 1024 * 1024),
         name="slope_and_modes",
-    )(layer_input, pre_act, out_grad, tables["swap"], tables["ends"], tables["place"], tables["forward"])
+    )(layer_input, pre_act, out_grad, tables["swap"], tables["ends"], tables["forward"])
 
 
 def middle_kernel(gain, norm, got_ref, gather_ref, weight_ref, halves_ref, spread_ref, mode_ref, sent_ref, stack):

time: 73.5 us -> 73 us (level)
  no operation moved by 1% of the time
where the time goes in v6:
time: 73 us; the launch traced here: 72.7 us
  starting transfers between devices  30.5 us (42%)
  waiting for transfers between devices  29.7 us (41%)
  Pallas kernels  6.94 us (10%)
  local copies, waits for them, and re-layouts  2.99 us (4%)
  matrix products  1.34 us (2%)
  between operations  0.8 us (1%)
    all_to_all x2, starting transfers between devices, exchange(): lax.all_to_all(sent, ('az', 'ax'), 0, 0, tiled=True)  30.5 us
    all_to_all x2, waiting for transfers between devices, exchange(): lax.all_to_all(sent, ('az', 'ax'), 0, 0, tiled=True)  29.7 us
    pallas_call x1, Pallas kernels, first(): pl.pallas_call(first_kernel, in_specs=[hbm] * 6, out_specs=[hbm] * 2, scr...  3.92 us
    pallas_call x1, Pallas kernels, last(): pl.pallas_call(last_kernel, in_specs=[vmem] * 6, out_specs=[hbm] * 3, scr...  1.55 us
    pallas_call x1, Pallas kernels, middle(): pl.pallas_call(functools.partial(middle_kernel, gain, norm), out_shape=[j...  1.47 us
  transfers between devices with their start and end apart: 2, of which 2 were waited for; matrix products, arithmetic and copies ran while one was open for 6% of the time, Pallas kernels for 0%

profile of v6, /device:TPU:1, one launch (start us, length us, event | category | flops | bytes accessed | tf_op | source)
XLA Modules:
  0.0 72.7 jit_solution(14859765690504532607)
XLA Ops:
  0.6 0.0 copy-start
  0.6 0.0 copy-start.3
  0.7 0.0 copy-start.5
  0.7 0.0 copy-start.6
  0.7 0.0 copy-start.8
  0.7 0.0 copy-start.1
  0.7 3.9 %slope_and_modes.1 = (bf16[64,2,16,128]{3,2,1,0:T(8,128)(2,1)}, bf16[1024,128]{1,0:T(8,128)(2,1)}) custom-call(bf16[64,2,16,128]{3,2,1,0:T(8,128)(2,1)} %layer_hbm.1, bf16[64,2,16,128]{3,2,1,0:T(8,128)(2,1)} %pre_hbm.1, bf16[64,2,16,128]{3,2,1,0:T(8,128)(2,1)} %grad_hbm.1, bf16[256,256]{1,0:T(8,128)(2,1)} %constant.30.clone.swap_hbm, ...), custom_call_target="tpu_custom_call" | custom-call | tf_op jit(solution)/shard_map/slope_and_modes/pallas_call | solution.py:167
  4.6 0.0 copy-start.2
  4.6 0.0 copy-start.4
  4.7 0.0 copy-start.7
  4.7 22.2 %all-to-all-start = ((bf16[512,2,128]{2,1,0:T(2,128)(2,1)}), bf16[512,2,128]{2,1,0:T(2,128)(2,1)S(1)}, u32[]{:S(2)}, u32[]{:S(2)}) async-start(bf16[512,2,128]{2,1,0:T(2,128)(2,1)} %bitcast.17), calls=%async_computation | async-start | bytes 524288 | tf_op jit(solution)/shard_map/all_to_all | solution.py:290
  26.9 0.0 copy-done
  26.9 1.3 %fusion = f32[2,16,128,64]{2,3,1,0:T(8,128)S(1)} fusion(bf16[64,2,16,128]{3,2,1,0:T(8,128)(2,1)} %get-tuple-element.16, bf16[64,64]{1,0:T(8,128)(2,1)S(1)} %copy-done), kind=kOutput, calls=%fused_computation.2 | convolution fusion | flops 33554432 | bytes 1581056 | tf_op jit(solution)/shard_map/io,oxtr->ixtr/dot_general | solution.py:315
  28.2 0.6 copy.26
  28.8 0.0 copy-done.8
  28.9 0.1 reshape.56
  28.9 15.2 %all-to-all-done = bf16[512,2,128]{2,1,0:T(2,128)(2,1)S(1)} async-done(((bf16[512,2,128]{2,1,0:T(2,128)(2,1)}), bf16[512,2,128]{2,1,0:T(2,128)(2,1)S(1)}, u32[]{:S(2)}, u32[]{:S(2)}) %all-to-all-start) | async-done | bytes 262176 | tf_op jit(solution)/shard_map/all_to_all | solution.py:290
  44.1 0.0 copy-done.3
  44.1 0.0 copy-done.5
  44.1 0.0 copy-done.6
  44.1 0.0 copy-done.1
  44.1 1.5 %modes_and_mixing.1 = (bf16[32,128]{1,0:T(8,128)(2,1)S(1)}, bf16[8,128,128]{2,1,0:T(8,128)(2,1)}) custom-call(bf16[1024,128]{1,0:T(8,128)(2,1)S(1)} %bitcast.15, bf16[80,1024]{1,0:T(8,128)(2,1)S(1)} %copy-done.3, bf16[1,32,4096]{2,1,0:T(8,128)(2,1)S(1)} %copy-done.1, bf16[256,128]{1,0:T(8,128)(2,1)S(1)} %copy-done.5, bf16[128,64]{1,0:T(8,128)(2,1)S(1)} %copy-done.6), custom_call_target="tpu_custom_call" | custom-call | tf_op jit(solution)/shard_map/modes_and_mixing/pallas_call | solution.py:218
  45.6 8.3 %all-to-all-start.1 = ((bf16[512,2,128]{2,1,0:T(2,128)(2,1)}), bf16[512,2,128]{2,1,0:T(2,128)(2,1)S(1)}, u32[]{:S(2)}, u32[]{:S(2)}) async-start(bf16[512,2,128]{2,1,0:T(2,128)(2,1)} %bitcast.2), calls=%async_computation.1 | async-start | bytes 524288 | tf_op jit(solution)/shard_map/all_to_all | solution.py:290
  54.0 0.3 multiply_convert_fusion
  54.3 1.2 %convert_element_type.30 = bf16[1,32,4096]{2,1,0:T(8,128)(2,1)} reshape(bf16[32,64,64]{2,1,0:T(8,128)(2,1)S(1)} %multiply_convert_fusion) | data formatting | bytes 524288 | tf_op jit(solution)/shard_map/convert_element_type | solution.py:311
  55.5 1.1 %dynamic-slice_bitcast_fusion.inverse_ref = bf16[256,1024]{1,0:T(8,128)(2,1)S(1)} fusion(bf16[8,256,1024]{2,1,0:T(8,128)(2,1)} %constant.36.clone, s32[]{:T(128)S(6)} %select_n.4), kind=kLoop, calls=%fused_computation.4 | loop fusion | bytes 1048580 | tf_op jit(solution)/shard_map/jit(dynamic_index_in_dim)/squeeze | solution.py:314
  56.6 14.6 %all-to-all-done.1 = bf16[512,2,128]{2,1,0:T(2,128)(2,1)S(1)} async-done(((bf16[512,2,128]{2,1,0:T(2,128)(2,1)}), bf16[512,2,128]{2,1,0:T(2,128)(2,1)S(1)}, u32[]{:S(2)}, u32[]{:S(2)}) %all-to-all-start.1) | async-done | bytes 262176 | tf_op jit(solution)/shard_map/all_to_all | solution.py:290
  71.1 0.0 copy-done.2
  71.1 0.0 copy-done.4
  71.1 0.0 copy-done.7
  71.2 1.6 %modes_to_field.1 = (bf16[64,2,16,128]{3,2,1,0:T(8,128)(2,1)}, f32[64,64]{1,0:T(8,128)}, f32[64]{0:T(128)}) custom-call(bf16[1024,128]{1,0:T(8,128)(2,1)S(1)} %bitcast.16, bf16[80,1024]{1,0:T(8,128)(2,1)S(1)} %copy-done.2, bf16[256,128]{1,0:T(8,128)(2,1)S(1)} %copy-done.4, f32[16,256]{1,0:T(8,128)S(1)} %copy-done.7, ...), custom_call_target="tpu_custom_call" | custom-call | tf_op jit(solution)/shard_map/modes_to_field/pallas_call | solution.py:265
  (2 shorter events, 0.0 us)
Async XLA Ops:
  0.6 26.2 %copy-start = (bf16[64,64]{1,0:T(8,128)(2,1)S(1)}, bf16[64,64]{1,0:T(8,128)(2,1)}, u32[]{:S(2)}) copy-start(bf16[64,64]{1,0:T(8,128)(2,1)} %param.19) | copy-start | bytes 24580
  0.6 43.5 %copy-start.3 = (bf16[80,1024]{1,0:T(8,128)(2,1)S(1)}, bf16[80,1024]{1,0:T(8,128)(2,1)}, u32[]{:S(2)}) copy-start(bf16[80,1024]{1,0:T(8,128)(2,1)} %constant.33.clone.gather_ref) | copy-start | bytes 491524
  0.7 43.5 %copy-start.5 = (bf16[256,128]{1,0:T(8,128)(2,1)S(1)}, bf16[256,128]{1,0:T(8,128)(2,1)}, u32[]{:S(2)}) copy-start(bf16[256,128]{1,0:T(8,128)(2,1)} %constant.34.clone.halves_ref) | copy-start | bytes 196612
  0.7 43.5 %copy-start.6 = (bf16[128,64]{1,0:T(8,128)(2,1)S(1)}, bf16[128,64]{1,0:T(8,128)(2,1)}, u32[]{:S(2)}) copy-start(bf16[128,64]{1,0:T(8,128)(2,1)} %constant.35.clone.spread_ref) | copy-start | bytes 49156
  0.7 28.1 %copy-start.8 = (bf16[1,2048]{1,0:T(2,128)(2,1)S(1)}, bf16[1,2048]{1,0:T(2,128)(2,1)}, u32[]{:S(2)}) copy-start(bf16[1,2048]{1,0:T(2,128)(2,1)} %param.21) | copy-start | bytes 12292
  0.7 43.4 %copy-start.1 = (bf16[1,32,4096]{2,1,0:T(8,128)(2,1)S(1)}, bf16[1,32,4096]{2,1,0:T(8,128)(2,1)}, u32[]{:S(2)}) copy-start(bf16[1,32,4096]{2,1,0:T(8,128)(2,1)} %weight_ref.1) | copy-start | bytes 786436
  4.6 66.5 %copy-start.2 = (bf16[80,1024]{1,0:T(8,128)(2,1)S(1)}, bf16[80,1024]{1,0:T(8,128)(2,1)}, u32[]{:S(2)}) copy-start(bf16[80,1024]{1,0:T(8,128)(2,1)} %constant.37.clone.pick_ref) | copy-start | bytes 491524
  4.6 66.5 %copy-start.4 = (bf16[256,128]{1,0:T(8,128)(2,1)S(1)}, bf16[256,128]{1,0:T(8,128)(2,1)}, u32[]{:S(2)}) copy-start(bf16[256,128]{1,0:T(8,128)(2,1)} %constant.38.clone.radial_ref) | copy-start | bytes 196612
  4.7 66.5 %copy-start.7 = (f32[16,256]{1,0:T(8,128)S(1)}, f32[16,256]{1,0:T(8,128)}, u32[]{:S(2)}) copy-start(f32[16,256]{1,0:T(8,128)} %constant.39.clone.same_ref) | copy-start | bytes 49156
  4.7 39.4 %all-to-all-start = ((bf16[512,2,128]{2,1,0:T(2,128)(2,1)}), bf16[512,2,128]{2,1,0:T(2,128)(2,1)S(1)}, u32[]{:S(2)}, u32[]{:S(2)}) async-start(bf16[512,2,128]{2,1,0:T(2,128)(2,1)} %bitcast.17), calls=%async_computation | async-start | bytes 524288 | tf_op jit(solution)/shard_map/all_to_all | solution.py:290
  45.6 25.5 %all-to-all-start.1 = ((bf16[512,2,128]{2,1,0:T(2,128)(2,1)}), bf16[512,2,128]{2,1,0:T(2,128)(2,1)S(1)}, u32[]{:S(2)}, u32[]{:S(2)}) async-start(bf16[512,2,128]{2,1,0:T(2,128)(2,1)} %bitcast.2), calls=%async_computation.1 | async-start | bytes 524288 | tf_op jit(solution)/shard_map/all_to_all | solution.py:290

commit v7 on v6

--- a/solution.py
+++ b/solution.py
@@ -42,11 +42,6 @@
     radial_table, axial_table = cosine_table(radial, MR), cosine_table(axial, MX)
     cycle_all = cycle_table(cycle, MT)
     tables = {}
-    swap = np.zeros((16, 16, 16, 16), np.float32)
-    for a in range(16):
-        for b in range(16):
-            swap[a, b, b, a] = 1.0
-    tables["swap"] = swap.reshape(256, 256)
     ends = np.zeros((32, radial), np.float32)
     ends[:MR] = radial_table.T
     ends[MR:] = 1.0
@@ -103,9 +98,9 @@
     return jnp.where(lane < 64, high, pltpu.roll(values - high, 64, 1))
 
 
-def first_kernel(layer_hbm, pre_hbm, grad_hbm, swap_hbm, ends_hbm, forward_hbm,
+def first_kernel(layer_hbm, pre_hbm, grad_hbm, ends_hbm, forward_hbm,
                  slope_hbm, sent_hbm, layer, pre, grad, slope, layer_rows, grad_rows, coefs,
-                 swap, ends, forward, sent, in_sem, out_sem, table_sem, sent_sem):
+                 ends, forward, sent, in_sem, out_sem, table_sem, sent_sem):
     chunks, blocks = in_sem.shape[0], sent_sem.shape[0]
     group, size = CH // chunks, sent.shape[0] // blocks
     copies = []
@@ -113,9 +108,9 @@
         part = pl.ds(c * group, group)
         pairs = ((pre_hbm, pre), (grad_hbm, grad), (layer_hbm, layer))
         copies.append([pltpu.make_async_copy(a.at[part], b.at[part], in_sem.at[c, n]) for n, (a, b) in enumerate(pairs)])
-    pairs = ((swap_hbm, swap), (ends_hbm, ends), (forward_hbm.at[lax.axis_index("az")], forward))
+    pairs = ((ends_hbm, ends), (forward_hbm.at[lax.axis_index("az")], forward))
     tables = [pltpu.make_async_copy(a, b, table_sem.at[n]) for n, (a, b) in enumerate(pairs)]
-    for copy in copies[0] + tables[:1] + sum(copies[1:], []) + tables[1:]:
+    for copy in sum(copies, []) + tables:
         copy.start()
     leaving = []
     for c in range(chunks):
@@ -126,18 +121,12 @@
         leaving.append(pltpu.make_async_copy(slope.at[part], slope_hbm.at[part], out_sem.at[c]))
         leaving[-1].start()
         copies[c][2].wait()
-        if c == 0:
-            tables[0].wait()
         for at in range(c * group, (c + 1) * group, 16):
             for x in range(2):
-                both = jnp.concatenate(
-                    [layer[at : at + 16, x].reshape(256, 128), slope[at : at + 16, x].reshape(256, 128)], axis=1
-                )
-                moved = dot_nn(swap[...], both).astype(BF)
                 rows = slice(x * CH + at, x * CH + at + 16)
-                layer_rows[:, rows, :] = moved[:, :128].reshape(16, 16, 128)
-                grad_rows[:, rows, :] = moved[:, 128:].reshape(16, 16, 128)
-    for copy in tables[1:]:
+                layer_rows[:, rows, :] = jnp.swapaxes(layer[at : at + 16, x], 0, 1)
+                grad_rows[:, rows, :] = jnp.swapaxes(slope[at : at + 16, x], 0, 1)
+    for copy in tables:
         copy.wait()
     point = dot_nt(
         jnp.concatenate([layer_rows[t] for t in range(16)], axis=1), jnp.concatenate([grad_rows[t] for t in range(16)], axis=1)
@@ -166,26 +155,25 @@
     hbm = pl.BlockSpec(memory_space=pl.ANY)
     return pl.pallas_call(
         first_kernel,
-        in_specs=[hbm] * 6,
+        in_specs=[hbm] * 5,
         out_specs=[hbm] * 2,
         scratch_shapes=[pltpu.VMEM(shape, BF)] * 4
         + [
             pltpu.VMEM((16, 128, 128), BF),
             pltpu.VMEM((16, 128, 128), BF),
             pltpu.VMEM((256, 128), BF),
-            pltpu.VMEM((256, 256), BF),
             pltpu.VMEM((32, 128), BF),
             pltpu.VMEM((1024, 384), BF),
             pltpu.VMEM((1024, 128), BF),
             pltpu.SemaphoreType.DMA((chunks, 3)),
             pltpu.SemaphoreType.DMA((chunks,)),
-            pltpu.SemaphoreType.DMA((3,)),
+            pltpu.SemaphoreType.DMA((2,)),
             pltpu.SemaphoreType.DMA((blocks,)),
         ],
         out_shape=[jax.ShapeDtypeStruct(shape, BF), jax.ShapeDtypeStruct((1024, 128), BF)],
         compiler_params=pltpu.CompilerParams(vmem_limit_bytes=60 * 1024 * 1024),
         name="slope_and_modes",
-    )(layer_input, pre_act, out_grad, tables["swap"], tables["ends"], tables["forward"])
+    )(layer_input, pre_act, out_grad, tables["ends"], tables["forward"])
 
 
 def middle_kernel(gain, norm, got_ref, gather_ref, weight_ref, halves_ref, spread_ref, mode_ref, sent_ref, stack):

time: 73 us -> 72.7 us (level)
  no operation moved by 1% of the time
where the time goes in v7:
time: 72.7 us; the launch traced here: 72.4 us
  starting transfers between devices  30.5 us (42%)
  waiting for transfers between devices  29.7 us (41%)
  Pallas kernels  6.65 us (9%)
  local copies, waits for them, and re-layouts  2.99 us (4%)
  matrix products  1.34 us (2%)
  between operations  0.8 us (1%)
    all_to_all x2, starting transfers between devices, exchange(): lax.all_to_all(sent, ('az', 'ax'), 0, 0, tiled=True)  30.5 us
    all_to_all x2, waiting for transfers between devices, exchange(): lax.all_to_all(sent, ('az', 'ax'), 0, 0, tiled=True)  29.7 us
    pallas_call x1, Pallas kernels, first(): pl.pallas_call(first_kernel, in_specs=[hbm] * 5, out_specs=[hbm] * 2, scr...  3.63 us
    pallas_call x1, Pallas kernels, last(): pl.pallas_call(last_kernel, in_specs=[vmem] * 6, out_specs=[hbm] * 3, scr...  1.56 us
    pallas_call x1, Pallas kernels, middle(): pl.pallas_call(functools.partial(middle_kernel, gain, norm), out_shape=[j...  1.47 us
  transfers between devices with their start and end apart: 2, of which 2 were waited for; matrix products, arithmetic and copies ran while one was open for 6% of the time, Pallas kernels for 0%

profile of v7, /device:TPU:1, one launch (start us, length us, event | category | flops | bytes accessed | tf_op | source)
XLA Modules:
  0.0 72.4 jit_solution(11022407615974479505)
XLA Ops:
  0.6 0.0 copy-start
  0.6 0.0 copy-start.3
  0.7 0.0 copy-start.5
  0.7 0.0 copy-start.6
  0.7 0.0 copy-start.8
  0.7 0.0 copy-start.1
  0.7 3.6 %slope_and_modes.1 = (bf16[64,2,16,128]{3,2,1,0:T(8,128)(2,1)}, bf16[1024,128]{1,0:T(8,128)(2,1)}) custom-call(bf16[64,2,16,128]{3,2,1,0:T(8,128)(2,1)} %layer_hbm.1, bf16[64,2,16,128]{3,2,1,0:T(8,128)(2,1)} %pre_hbm.1, bf16[64,2,16,128]{3,2,1,0:T(8,128)(2,1)} %grad_hbm.1, bf16[32,128]{1,0:T(8,128)(2,1)} %constant.28.clone.ends_hbm, ...), custom_call_target="tpu_custom_call" | custom-call | tf_op jit(solution)/shard_map/slope_and_modes/pallas_call | solution.py:156
  4.3 0.0 copy-start.2
  4.4 0.0 copy-start.4
  4.4 0.0 copy-start.7
  4.4 22.2 %all-to-all-start = ((bf16[512,2,128]{2,1,0:T(2,128)(2,1)}), bf16[512,2,128]{2,1,0:T(2,128)(2,1)S(1)}, u32[]{:S(2)}, u32[]{:S(2)}) async-start(bf16[512,2,128]{2,1,0:T(2,128)(2,1)} %bitcast.17), calls=%async_computation | async-start | bytes 524288 | tf_op jit(solution)/shard_map/all_to_all | solution.py:278
  26.6 0.0 copy-done
  26.6 1.3 %fusion = f32[2,16,128,64]{2,3,1,0:T(8,128)S(1)} fusion(bf16[64,2,16,128]{3,2,1,0:T(8,128)(2,1)} %get-tuple-element.16, bf16[64,64]{1,0:T(8,128)(2,1)S(1)} %copy-done), kind=kOutput, calls=%fused_computation.2 | convolution fusion | flops 33554432 | bytes 1581056 | tf_op jit(solution)/shard_map/io,oxtr->ixtr/dot_general | solution.py:303
  27.9 0.6 copy.25
  28.5 0.0 copy-done.8
  28.6 0.1 reshape.56
  28.6 15.2 %all-to-all-done = bf16[512,2,128]{2,1,0:T(2,128)(2,1)S(1)} async-done(((bf16[512,2,128]{2,1,0:T(2,128)(2,1)}), bf16[512,2,128]{2,1,0:T(2,128)(2,1)S(1)}, u32[]{:S(2)}, u32[]{:S(2)}) %all-to-all-start) | async-done | bytes 262176 | tf_op jit(solution)/shard_map/all_to_all | solution.py:278
  43.8 0.0 copy-done.3
  43.8 0.0 copy-done.5
  43.8 0.0 copy-done.6
  43.8 0.0 copy-done.1
  43.8 1.5 %modes_and_mixing.1 = (bf16[32,128]{1,0:T(8,128)(2,1)S(1)}, bf16[8,128,128]{2,1,0:T(8,128)(2,1)}) custom-call(bf16[1024,128]{1,0:T(8,128)(2,1)S(1)} %bitcast.15, bf16[80,1024]{1,0:T(8,128)(2,1)S(1)} %copy-done.3, bf16[1,32,4096]{2,1,0:T(8,128)(2,1)S(1)} %copy-done.1, bf16[256,128]{1,0:T(8,128)(2,1)S(1)} %copy-done.5, bf16[128,64]{1,0:T(8,128)(2,1)S(1)} %copy-done.6), custom_call_target="tpu_custom_call" | custom-call | tf_op jit(solution)/shard_map/modes_and_mixing/pallas_call | solution.py:206
  45.3 8.3 %all-to-all-start.1 = ((bf16[512,2,128]{2,1,0:T(2,128)(2,1)}), bf16[512,2,128]{2,1,0:T(2,128)(2,1)S(1)}, u32[]{:S(2)}, u32[]{:S(2)}) async-start(bf16[512,2,128]{2,1,0:T(2,128)(2,1)} %bitcast.2), calls=%async_computation.1 | async-start | bytes 524288 | tf_op jit(solution)/shard_map/all_to_all | solution.py:278
  53.7 0.3 multiply_convert_fusion
  54.0 1.2 %convert_element_type.30 = bf16[1,32,4096]{2,1,0:T(8,128)(2,1)} reshape(bf16[32,64,64]{2,1,0:T(8,128)(2,1)S(1)} %multiply_convert_fusion) | data formatting | bytes 524288 | tf_op jit(solution)/shard_map/convert_element_type | solution.py:299
  55.2 1.1 %dynamic-slice_bitcast_fusion.inverse_ref = bf16[256,1024]{1,0:T(8,128)(2,1)S(1)} fusion(bf16[8,256,1024]{2,1,0:T(8,128)(2,1)} %constant.33.clone, s32[]{:T(128)S(6)} %select_n.4), kind=kLoop, calls=%fused_computation.4 | loop fusion | bytes 1048580 | tf_op jit(solution)/shard_map/jit(dynamic_index_in_dim)/squeeze | solution.py:302
  56.3 14.6 %all-to-all-done.1 = bf16[512,2,128]{2,1,0:T(2,128)(2,1)S(1)} async-done(((bf16[512,2,128]{2,1,0:T(2,128)(2,1)}), bf16[512,2,128]{2,1,0:T(2,128)(2,1)S(1)}, u32[]{:S(2)}, u32[]{:S(2)}) %all-to-all-start.1) | async-done | bytes 262176 | tf_op jit(solution)/shard_map/all_to_all | solution.py:278
  70.8 0.0 copy-done.2
  70.9 0.0 copy-done.4
  70.9 0.0 copy-done.7
  70.9 1.6 %modes_to_field.1 = (bf16[64,2,16,128]{3,2,1,0:T(8,128)(2,1)}, f32[64,64]{1,0:T(8,128)}, f32[64]{0:T(128)}) custom-call(bf16[1024,128]{1,0:T(8,128)(2,1)S(1)} %bitcast.16, bf16[80,1024]{1,0:T(8,128)(2,1)S(1)} %copy-done.2, bf16[256,128]{1,0:T(8,128)(2,1)S(1)} %copy-done.4, f32[16,256]{1,0:T(8,128)S(1)} %copy-done.7, ...), custom_call_target="tpu_custom_call" | custom-call | tf_op jit(solution)/shard_map/modes_to_field/pallas_call | solution.py:253
  (2 shorter events, 0.0 us)
Async XLA Ops:
  0.6 25.9 %copy-start = (bf16[64,64]{1,0:T(8,128)(2,1)S(1)}, bf16[64,64]{1,0:T(8,128)(2,1)}, u32[]{:S(2)}) copy-start(bf16[64,64]{1,0:T(8,128)(2,1)} %param.18) | copy-start | bytes 24580
  0.6 43.2 %copy-start.3 = (bf16[80,1024]{1,0:T(8,128)(2,1)S(1)}, bf16[80,1024]{1,0:T(8,128)(2,1)}, u32[]{:S(2)}) copy-start(bf16[80,1024]{1,0:T(8,128)(2,1)} %constant.30.clone.gather_ref) | copy-start | bytes 491524
  0.7 43.2 %copy-start.5 = (bf16[256,128]{1,0:T(8,128)(2,1)S(1)}, bf16[256,128]{1,0:T(8,128)(2,1)}, u32[]{:S(2)}) copy-start(bf16[256,128]{1,0:T(8,128)(2,1)} %constant.31.clone.halves_ref) | copy-start | bytes 196612
  0.7 43.2 %copy-start.6 = (bf16[128,64]{1,0:T(8,128)(2,1)S(1)}, bf16[128,64]{1,0:T(8,128)(2,1)}, u32[]{:S(2)}) copy-start(bf16[128,64]{1,0:T(8,128)(2,1)} %constant.32.clone.spread_ref) | copy-start | bytes 49156
  0.7 27.9 %copy-start.8 = (bf16[1,2048]{1,0:T(2,128)(2,1)S(1)}, bf16[1,2048]{1,0:T(2,128)(2,1)}, u32[]{:S(2)}) copy-start(bf16[1,2048]{1,0:T(2,128)(2,1)} %param.20) | copy-start | bytes 12292
  0.7 43.1 %copy-start.1 = (bf16[1,32,4096]{2,1,0:T(8,128)(2,1)S(1)}, bf16[1,32,4096]{2,1,0:T(8,128)(2,1)}, u32[]{:S(2)}) copy-start(bf16[1,32,4096]{2,1,0:T(8,128)(2,1)} %weight_ref.1) | copy-start | bytes 786436
  4.3 66.5 %copy-start.2 = (bf16[80,1024]{1,0:T(8,128)(2,1)S(1)}, bf16[80,1024]{1,0:T(8,128)(2,1)}, u32[]{:S(2)}) copy-start(bf16[80,1024]{1,0:T(8,128)(2,1)} %constant.34.clone.pick_ref) | copy-start | bytes 491524
  4.4 66.5 %copy-start.4 = (bf16[256,128]{1,0:T(8,128)(2,1)S(1)}, bf16[256,128]{1,0:T(8,128)(2,1)}, u32[]{:S(2)}) copy-start(bf16[256,128]{1,0:T(8,128)(2,1)} %constant.35.clone.radial_ref) | copy-start | bytes 196612
  4.4 66.5 %copy-start.7 = (f32[16,256]{1,0:T(8,128)S(1)}, f32[16,256]{1,0:T(8,128)}, u32[]{:S(2)}) copy-start(f32[16,256]{1,0:T(8,128)} %constant.36.clone.same_ref) | copy-start | bytes 49156
  4.4 39.4 %all-to-all-start = ((bf16[512,2,128]{2,1,0:T(2,128)(2,1)}), bf16[512,2,128]{2,1,0:T(2,128)(2,1)S(1)}, u32[]{:S(2)}, u32[]{:S(2)}) async-start(bf16[512,2,128]{2,1,0:T(2,128)(2,1)} %bitcast.17), calls=%async_computation | async-start | bytes 524288 | tf_op jit(solution)/shard_map/all_to_all | solution.py:278
  45.3 25.5 %all-to-all-start.1 = ((bf16[512,2,128]{2,1,0:T(2,128)(2,1)}), bf16[512,2,128]{2,1,0:T(2,128)(2,1)S(1)}, u32[]{:S(2)}, u32[]{:S(2)}) async-start(bf16[512,2,128]{2,1,0:T(2,128)(2,1)} %bitcast.2), calls=%async_computation.1 | async-start | bytes 524288 | tf_op jit(solution)/shard_map/all_to_all | solution.py:278

commit v8 on v7

--- a/solution.py
+++ b/solution.py
@@ -188,10 +188,14 @@
         high = product.astype(BF)
         stack[c * 32 : (c + 1) * 32, :128] = high
         stack[c * 32 : (c + 1) * 32, 128:] = (product - high.astype(F32)).astype(BF)
-    summed = dot_nn(stack[...], halves_ref[...])
-    coef = jnp.zeros((32, 128), F32)
-    for c in range(32):
-        coef = jnp.where(lane % 64 == c, summed[c * 32 : (c + 1) * 32], coef)
+    chains = []
+    for start in range(0, 32, 8):
+        summed = dot_nn(stack[start * 32 : start * 32 + 256], halves_ref[...])
+        coef = jnp.zeros((32, 128), F32)
+        for c in range(8):
+            coef = jnp.where(lane % 64 == start + c, summed[c * 32 : (c + 1) * 32], coef)
+        chains.append(coef)
+    coef = (chains[0] + chains[1]) + (chains[2] + chains[3])
     coef = jnp.concatenate([coef, pltpu.roll(coef, 32, 1)], axis=0).astype(BF)
     slabs = dot_nn(spread_ref[...], coef)
     sums = full[64:80]

time: 72.7 us -> 72.7 us (level)
  no operation moved by 1% of the time
where the time goes in v8:
time: 72.7 us; the launch traced here: 72.4 us
  starting transfers between devices  30.5 us (42%)
  waiting for transfers between devices  29.7 us (41%)
  Pallas kernels  6.66 us (9%)
  local copies, waits for them, and re-layouts  2.99 us (4%)
  matrix products  1.34 us (2%)
  between operations  0.8 us (1%)
    all_to_all x2, starting transfers between devices, exchange(): lax.all_to_all(sent, ('az', 'ax'), 0, 0, tiled=True)  30.5 us
    all_to_all x2, waiting for transfers between devices, exchange(): lax.all_to_all(sent, ('az', 'ax'), 0, 0, tiled=True)  29.7 us
    pallas_call x1, Pallas kernels, first(): pl.pallas_call(first_kernel, in_specs=[hbm] * 5, out_specs=[hbm] * 2, scr...  3.63 us
    pallas_call x1, Pallas kernels, last(): pl.pallas_call(last_kernel, in_specs=[vmem] * 6, out_specs=[hbm] * 3, scr...  1.56 us
    pallas_call x1, Pallas kernels, middle(): pl.pallas_call(functools.partial(middle_kernel, gain, norm), out_shape=[j...  1.47 us
  transfers between devices with their start and end apart: 2, of which 2 were waited for; matrix products, arithmetic and copies ran while one was open for 6% of the time, Pallas kernels for 0%

profile of v8, /device:TPU:1, one launch (start us, length us, event | category | flops | bytes accessed | tf_op | source)
XLA Modules:
  0.0 72.4 jit_solution(18348564706637857290)
XLA Ops:
  0.6 0.0 copy-start
  0.6 0.0 copy-start.3
  0.7 0.0 copy-start.5
  0.7 0.0 copy-start.6
  0.7 0.0 copy-start.8
  0.7 0.0 copy-start.1
  0.7 3.6 %slope_and_modes.1 = (bf16[64,2,16,128]{3,2,1,0:T(8,128)(2,1)}, bf16[1024,128]{1,0:T(8,128)(2,1)}) custom-call(bf16[64,2,16,128]{3,2,1,0:T(8,128)(2,1)} %layer_hbm.1, bf16[64,2,16,128]{3,2,1,0:T(8,128)(2,1)} %pre_hbm.1, bf16[64,2,16,128]{3,2,1,0:T(8,128)(2,1)} %grad_hbm.1, bf16[32,128]{1,0:T(8,128)(2,1)} %constant.28.clone.ends_hbm, ...), custom_call_target="tpu_custom_call" | custom-call | tf_op jit(solution)/shard_map/slope_and_modes/pallas_call | solution.py:156
  4.3 0.0 copy-start.2
  4.4 0.0 copy-start.4
  4.4 0.0 copy-start.7
  4.4 22.2 %all-to-all-start = ((bf16[512,2,128]{2,1,0:T(2,128)(2,1)}), bf16[512,2,128]{2,1,0:T(2,128)(2,1)S(1)}, u32[]{:S(2)}, u32[]{:S(2)}) async-start(bf16[512,2,128]{2,1,0:T(2,128)(2,1)} %bitcast.17), calls=%async_computation | async-start | bytes 524288 | tf_op jit(solution)/shard_map/all_to_all | solution.py:282
  26.6 0.0 copy-done
  26.6 1.3 %fusion = f32[2,16,128,64]{2,3,1,0:T(8,128)S(1)} fusion(bf16[64,2,16,128]{3,2,1,0:T(8,128)(2,1)} %get-tuple-element.16, bf16[64,64]{1,0:T(8,128)(2,1)S(1)} %copy-done), kind=kOutput, calls=%fused_computation.2 | convolution fusion | flops 33554432 | bytes 1581056 | tf_op jit(solution)/shard_map/io,oxtr->ixtr/dot_general | solution.py:307
  27.9 0.6 copy.25
  28.5 0.0 copy-done.8
  28.6 0.1 reshape.56
  28.6 15.2 %all-to-all-done = bf16[512,2,128]{2,1,0:T(2,128)(2,1)S(1)} async-done(((bf16[512,2,128]{2,1,0:T(2,128)(2,1)}), bf16[512,2,128]{2,1,0:T(2,128)(2,1)S(1)}, u32[]{:S(2)}, u32[]{:S(2)}) %all-to-all-start) | async-done | bytes 262176 | tf_op jit(solution)/shard_map/all_to_all | solution.py:282
  43.8 0.0 copy-done.3
  43.8 0.0 copy-done.5
  43.8 0.0 copy-done.6
  43.8 0.0 copy-done.1
  43.8 1.5 %modes_and_mixing.1 = (bf16[32,128]{1,0:T(8,128)(2,1)S(1)}, bf16[8,128,128]{2,1,0:T(8,128)(2,1)}) custom-call(bf16[1024,128]{1,0:T(8,128)(2,1)S(1)} %bitcast.15, bf16[80,1024]{1,0:T(8,128)(2,1)S(1)} %copy-done.3, bf16[1,32,4096]{2,1,0:T(8,128)(2,1)S(1)} %copy-done.1, bf16[256,128]{1,0:T(8,128)(2,1)S(1)} %copy-done.5, bf16[128,64]{1,0:T(8,128)(2,1)S(1)} %copy-done.6), custom_call_target="tpu_custom_call" | custom-call | tf_op jit(solution)/shard_map/modes_and_mixing/pallas_call | solution.py:210
  45.3 8.3 %all-to-all-start.1 = ((bf16[512,2,128]{2,1,0:T(2,128)(2,1)}), bf16[512,2,128]{2,1,0:T(2,128)(2,1)S(1)}, u32[]{:S(2)}, u32[]{:S(2)}) async-start(bf16[512,2,128]{2,1,0:T(2,128)(2,1)} %bitcast.2), calls=%async_computation.1 | async-start | bytes 524288 | tf_op jit(solution)/shard_map/all_to_all | solution.py:282
  53.7 0.3 multiply_convert_fusion
  54.0 1.2 %convert_element_type.30 = bf16[1,32,4096]{2,1,0:T(8,128)(2,1)} reshape(bf16[32,64,64]{2,1,0:T(8,128)(2,1)S(1)} %multiply_convert_fusion) | data formatting | bytes 524288 | tf_op jit(solution)/shard_map/convert_element_type | solution.py:303
  55.2 1.1 %dynamic-slice_bitcast_fusion.inverse_ref = bf16[256,1024]{1,0:T(8,128)(2,1)S(1)} fusion(bf16[8,256,1024]{2,1,0:T(8,128)(2,1)} %constant.33.clone, s32[]{:T(128)S(6)} %select_n.4), kind=kLoop, calls=%fused_computation.4 | loop fusion | bytes 1048580 | tf_op jit(solution)/shard_map/jit(dynamic_index_in_dim)/squeeze | solution.py:306
  56.3 14.6 %all-to-all-done.1 = bf16[512,2,128]{2,1,0:T(2,128)(2,1)S(1)} async-done(((bf16[512,2,128]{2,1,0:T(2,128)(2,1)}), bf16[512,2,128]{2,1,0:T(2,128)(2,1)S(1)}, u32[]{:S(2)}, u32[]{:S(2)}) %all-to-all-start.1) | async-done | bytes 262176 | tf_op jit(solution)/shard_map/all_to_all | solution.py:282
  70.9 0.0 copy-done.2
  70.9 0.0 copy-done.4
  70.9 0.0 copy-done.7
  70.9 1.6 %modes_to_field.1 = (bf16[64,2,16,128]{3,2,1,0:T(8,128)(2,1)}, f32[64,64]{1,0:T(8,128)}, f32[64]{0:T(128)}) custom-call(bf16[1024,128]{1,0:T(8,128)(2,1)S(1)} %bitcast.16, bf16[80,1024]{1,0:T(8,128)(2,1)S(1)} %copy-done.2, bf16[256,128]{1,0:T(8,128)(2,1)S(1)} %copy-done.4, f32[16,256]{1,0:T(8,128)S(1)} %copy-done.7, ...), custom_call_target="tpu_custom_call" | custom-call | tf_op jit(solution)/shard_map/modes_to_field/pallas_call | solution.py:257
  (2 shorter events, 0.0 us)
Async XLA Ops:
  0.6 25.9 %copy-start = (bf16[64,64]{1,0:T(8,128)(2,1)S(1)}, bf16[64,64]{1,0:T(8,128)(2,1)}, u32[]{:S(2)}) copy-start(bf16[64,64]{1,0:T(8,128)(2,1)} %param.18) | copy-start | bytes 24580
  0.6 43.2 %copy-start.3 = (bf16[80,1024]{1,0:T(8,128)(2,1)S(1)}, bf16[80,1024]{1,0:T(8,128)(2,1)}, u32[]{:S(2)}) copy-start(bf16[80,1024]{1,0:T(8,128)(2,1)} %constant.30.clone.gather_ref) | copy-start | bytes 491524
  0.7 43.2 %copy-start.5 = (bf16[256,128]{1,0:T(8,128)(2,1)S(1)}, bf16[256,128]{1,0:T(8,128)(2,1)}, u32[]{:S(2)}) copy-start(bf16[256,128]{1,0:T(8,128)(2,1)} %constant.31.clone.halves_ref) | copy-start | bytes 196612
  0.7 43.2 %copy-start.6 = (bf16[128,64]{1,0:T(8,128)(2,1)S(1)}, bf16[128,64]{1,0:T(8,128)(2,1)}, u32[]{:S(2)}) copy-start(bf16[128,64]{1,0:T(8,128)(2,1)} %constant.32.clone.spread_ref) | copy-start | bytes 49156
  0.7 27.9 %copy-start.8 = (bf16[1,2048]{1,0:T(2,128)(2,1)S(1)}, bf16[1,2048]{1,0:T(2,128)(2,1)}, u32[]{:S(2)}) copy-start(bf16[1,2048]{1,0:T(2,128)(2,1)} %param.20) | copy-start | bytes 12292
  0.7 43.1 %copy-start.1 = (bf16[1,32,4096]{2,1,0:T(8,128)(2,1)S(1)}, bf16[1,32,4096]{2,1,0:T(8,128)(2,1)}, u32[]{:S(2)}) copy-start(bf16[1,32,4096]{2,1,0:T(8,128)(2,1)} %weight_ref.1) | copy-start | bytes 786436
  4.3 66.5 %copy-start.2 = (bf16[80,1024]{1,0:T(8,128)(2,1)S(1)}, bf16[80,1024]{1,0:T(8,128)(2,1)}, u32[]{:S(2)}) copy-start(bf16[80,1024]{1,0:T(8,128)(2,1)} %constant.34.clone.pick_ref) | copy-start | bytes 491524
  4.4 66.5 %copy-start.4 = (bf16[256,128]{1,0:T(8,128)(2,1)S(1)}, bf16[256,128]{1,0:T(8,128)(2,1)}, u32[]{:S(2)}) copy-start(bf16[256,128]{1,0:T(8,128)(2,1)} %constant.35.clone.radial_ref) | copy-start | bytes 196612
  4.4 66.5 %copy-start.7 = (f32[16,256]{1,0:T(8,128)S(1)}, f32[16,256]{1,0:T(8,128)}, u32[]{:S(2)}) copy-start(f32[16,256]{1,0:T(8,128)} %constant.36.clone.same_ref) | copy-start | bytes 49156
  4.4 39.4 %all-to-all-start = ((bf16[512,2,128]{2,1,0:T(2,128)(2,1)}), bf16[512,2,128]{2,1,0:T(2,128)(2,1)S(1)}, u32[]{:S(2)}, u32[]{:S(2)}) async-start(bf16[512,2,128]{2,1,0:T(2,128)(2,1)} %bitcast.17), calls=%async_computation | async-start | bytes 524288 | tf_op jit(solution)/shard_map/all_to_all | solution.py:282
  45.3 25.5 %all-to-all-start.1 = ((bf16[512,2,128]{2,1,0:T(2,128)(2,1)}), bf16[512,2,128]{2,1,0:T(2,128)(2,1)S(1)}, u32[]{:S(2)}, u32[]{:S(2)}) async-start(bf16[512,2,128]{2,1,0:T(2,128)(2,1)} %bitcast.2), calls=%async_computation.1 | async-start | bytes 524288 | tf_op jit(solution)/shard_map/all_to_all | solution.py:282
